TPU v7x, 32 devices: a whole 2x2x4 slice. The times are simulated.
32 devices in a mesh: rows: 16 (over z, y, x), inner: 2 (over core).
Axes of the slice: x: 2, y: 2, z: 4, core: 2. Of those that a mesh axis runs over, the one named last changes fastest.
Arguments:
- hidden: bfloat16 [16, 1568, 384], P('rows', 'inner'), may hold values from -6 to 6
- kept: int32 [16, 392], P('rows'), may hold values from 0 to 1567, as said below
- counts: int32 [16], P('rows'), may hold values from 196 to 392, as said below
- norm_gain: float32 [384], replicated, may hold values from 0.5 to 1.5
- in_weight: bfloat16 [2, 384, 768], P(None, None, 'inner'), may hold values from -0.3125 to 0.3125
- conv_weight: bfloat16 [2, 4, 768], P(None, None, 'inner'), may hold values from -3 to 3
- conv_bias: float32 [2, 768], P(None, 'inner'), may hold values from -3 to 3
- x_weight: bfloat16 [2, 768, 56], P(None, 'inner'), may hold values from -0.21875 to 0.21875
- dt_weight: bfloat16 [2, 24, 768], P(None, None, 'inner'), may hold values from -1.25 to 1.25
- dt_bias: float32 [2, 768], P(None, 'inner'), may hold values from -6 to -1
- a_log: float32 [2, 16, 768], P(None, None, 'inner'), may hold values from 0 to 2.77
- skip_gain: float32 [2, 768], P(None, 'inner'), may hold values from 0.5 to 1.5
- out_weight: bfloat16 [768, 384], P('inner'), may hold values from -0.21875 to 0.21875
- cotangent: bfloat16 [16, 392, 384], P('rows', 'inner'), may hold values from -6 to 6
Outputs:
- output: bfloat16 [16, 392, 384], P('rows', 'inner')
- hidden_grad: bfloat16 [16, 1568, 384], P('rows', 'inner')
- norm_gain_grad: float32 [384], P('inner')
- in_weight_grad: float32 [2, 384, 768], P(None, None, 'inner')
- conv_weight_grad: float32 [2, 4, 768], P(None, None, 'inner')
- conv_bias_grad: float32 [2, 768], P(None, 'inner')
- x_weight_grad: float32 [2, 768, 56], P(None, 'inner')
- dt_weight_grad: float32 [2, 24, 768], P(None, None, 'inner')
- dt_bias_grad: float32 [2, 768], P(None, 'inner')
- a_log_grad: float32 [2, 16, 768], P(None, None, 'inner')
- skip_gain_grad: float32 [2, 768], P(None, 'inner')
- out_weight_grad: float32 [768, 384], P('inner')
- dt_mean: float32 [2, 768], P(None, 'inner')
- dt_var: float32 [2, 768], P(None, 'inner')
Inputs may be any that keep to these rules, and one draw needn't show every extreme that they name: `kept`: in clip c, slots 0 to counts[c] - 1 hold distinct positions of that clip in increasing order; the remaining slots hold other distinct positions and are not used. `counts`: kept tokens of each clip; some clip keeps 392.
All inputs are finite; a program needn't handle non-finite values.
Results may differ from a plain program's by a relative error of at most 0.011.
Values may be sent and summed in bfloat16 or wider, within the bound.
A program may use at most 128 MiB of HBM per device.

v0:
```python
import functools

import jax
import jax.numpy as jnp
from jax import lax
from jax.experimental import pallas as pl
from jax.experimental.pallas import tpu as pltpu
from jax.sharding import PartitionSpec as P

EPSILON = 1e-05
BLOCK = 16
LOG2E = 1.4426950408889634
MESH = pl.DeviceIdType.MESH
F32 = jnp.float32
BF16 = jnp.bfloat16


def dot(left, right):
    return jnp.dot(left, right, preferred_element_type=F32)


def dot_nt(left, right):
    return lax.dot_general(left, right, (((1,), (1,)), ((), ())), preferred_element_type=F32)


def dot_tn(left, right):
    return lax.dot_general(left, right, (((0,), (0,)), ((), ())), preferred_element_type=F32)


def iota(shape, axis):
    return lax.broadcasted_iota(jnp.int32, shape, axis)


def round_up(value, unit):
    return (value + unit - 1) // unit * unit


def block_kernel(
    sizes,
    hidden,
    kept,
    counts,
    norm_gain,
    in_weight,
    conv_weight,
    conv_bias,
    x_weight,
    dt_weight,
    dt_bias,
    a_log,
    skip_gain,
    out_weight,
    cotangent,
    output,
    hidden_grad,
    gain_grad,
    in_grad,
    conv_w_grad,
    conv_b_grad,
    xw_grad,
    dtw_grad,
    dtb_grad,
    alog_grad,
    skip_grad,
    out_grad,
    dt_sums,
    picked,
    picked_in,
    cot_pair,
    gout_f,
    gout,
    gathered,
    inverse,
    normed,
    px,
    pz,
    slope,
    act,
    xw_cat,
    dtw_pad,
    rates2,
    rates,
    part,
    part_in,
    proj,
    projb,
    delta,
    sig,
    u,
    up,
    gate,
    zslope,
    zgrad,
    gated,
    terms,
    terms_pair,
    terms_in,
    blkm,
    turned_rows,
    sel,
    states,
    ys,
    adj_0,
    adj_1,
    car_0,
    car_1,
    bsum_0,
    bsum_1,
    csum_0,
    csum_1,
    s1,
    cas,
    pgm,
    soft,
    actg,
    pgrad,
    pgrad_in,
    pgb,
    cgrad,
    xgrad,
    npart,
    npart_b,
    npart_in,
    sgrad,
    send_sem,
    recv_sem,
):
    half_full, width, slots, padded, half_slots, half_pad, inner_w, rank, state = sizes
    blocks = padded // BLOCK
    inner = lax.axis_index("inner")
    peer = 1 - inner

    def remote(source, target, index):
        return pltpu.make_async_remote_copy(
            src_ref=source,
            dst_ref=target,
            send_sem=send_sem.at[index],
            recv_sem=recv_sem.at[index],
            device_id={"inner": peer},
            device_id_type=MESH,
        )

    def rows_at(block):
        return pl.ds(pl.multiple_of(block * BLOCK, BLOCK), BLOCK)

    def each_block(body, unroll=5):
        def step(block, carry):
            body(block)
            return carry

        lax.fori_loop(0, blocks, step, 0, unroll=unroll)

    barrier = pltpu.get_barrier_semaphore()
    pl.semaphore_signal(barrier, inc=1, device_id={"inner": peer}, device_id_type=MESH)

    count = counts[0]
    kept_row = kept[...].astype(F32)
    first = (inner * half_full).astype(F32)

    own_cot = cotangent[...].astype(F32)
    cot_rows = iota((half_slots, 1), 0) + inner * half_slots
    own_cot = jnp.where(cot_rows < count, own_cot, 0.0)
    cot_full = jnp.concatenate([own_cot, jnp.zeros((half_pad - half_slots, width), F32)], 0)
    cot_pair[pl.ds(inner, 1)] = cot_full.astype(BF16)[None]

    def pick_rows(block):
        rows = iota((BLOCK, slots), 0) + block * BLOCK
        mine = jnp.where(rows == iota((BLOCK, slots), 1), kept_row, 0.0)
        place = jnp.sum(mine, axis=1, keepdims=True) - first
        slot = iota((BLOCK, 1), 0) + block * BLOCK
        place = jnp.where(slot < count, place, -1.0)
        column = iota((BLOCK, half_full), 1).astype(F32)
        chosen = jnp.where(place == column, 1.0, 0.0).astype(BF16)
        picked[rows_at(block), :] = dot(chosen, hidden[...]).astype(BF16)

    each_block(pick_rows, 1)
    pl.semaphore_wait(barrier, 1)
    send_pick = remote(picked, picked_in, 0)
    send_pick.start()
    send_cot = remote(cot_pair.at[inner], cot_pair.at[inner], 1)
    send_cot.start()

    pad_lane = jnp.zeros((inner_w, 64 - rank - 2 * state), F32)
    for r in range(2):
        mine = jnp.concatenate([x_weight[r].astype(F32), pad_lane], 1)
        other = jnp.zeros((inner_w, 64), F32)
        both = [mine, other] if r == 0 else [other, mine]
        xw_cat[r] = jnp.concatenate(both, 1).astype(BF16)
        low = dt_weight[r].astype(F32)
        parts = [low, jnp.zeros((128 - 64 * r - rank, inner_w), F32)]
        if r:
            parts = [jnp.zeros((64 * r, inner_w), F32)] + parts
        dtw_pad[r] = jnp.concatenate(parts, 0).astype(BF16)
        rate = -jnp.exp(a_log[r])
        rates[r] = rate
        rates2[r] = rate * LOG2E
    lane = iota((128, 1024), 1)
    chunk = lane // 256
    start = jnp.where(
        chunk == 0,
        rank,
        jnp.where(chunk == 1, rank + state, jnp.where(chunk == 2, 64 + rank, 64 + rank + state)),
    )
    sel[...] = jnp.where(iota((128, 1024), 0) == start + lane % state, 1.0, 0.0).astype(BF16)
    zero_rows = jnp.zeros((8, inner_w), F32)
    px[0:8, :] = zero_rows
    px[8 + padded : 16 + padded, :] = zero_rows
    for r in range(2):
        cgrad[r, 0:8, :] = zero_rows
        cgrad[r, 8 + padded : 16 + padded, :] = zero_rows
    states[0, 0:16, :] = jnp.zeros((16, inner_w), BF16)
    states[1, padded * 16 : padded * 16 + 16, :] = jnp.zeros((16, inner_w), BF16)

    send_pick.wait()
    gain = norm_gain[...]

    def norm_rows(block):
        rows = rows_at(block)
        held = picked[rows, :].astype(F32) + picked_in[rows, :].astype(F32)
        gathered[rows, :] = held
        scale = lax.rsqrt(jnp.sum(held * held, axis=1, keepdims=True) / width + EPSILON)
        inverse[rows, :] = scale
        normed[rows, :] = (held * scale * gain).astype(BF16)

    each_block(norm_rows)
    px[8 : 8 + padded, :] = dot(normed[...], in_weight[0])
    pz[...] = dot(normed[...], in_weight[1])

    taps = conv_weight[...].astype(F32)

    def conv_rows(block):
        base = pl.multiple_of(block * BLOCK, BLOCK)
        rows = rows_at(block)
        slot = iota((BLOCK, 1), 0) + block * BLOCK
        valid = jnp.where(slot < count, 1.0, 0.0)
        window = px[pl.ds(base, BLOCK + 16), :]
        for r in range(2):
            total = conv_bias[r : r + 1, :]
            for k in range(4):
                shift = k - 3 if r == 0 else 3 - k
                total = total + taps[r, k : k + 1, :] * window[8 + shift : 8 + shift + BLOCK, :]
            logistic = jax.nn.sigmoid(total)
            act[r, rows, :] = (total * logistic * valid).astype(BF16)
            slope[r, rows, :] = logistic * (1.0 + total * (1.0 - logistic)) * valid

    each_block(conv_rows, 1)
    part[...] = dot(act[0], xw_cat[0]) + dot(act[1], xw_cat[1])
    send_part = remote(part, part_in, 2)
    send_part.start()

    send_cot.wait()
    gout_f[0:half_pad, :] = cot_pair[0].astype(F32)
    gout_f[half_pad:, :] = jnp.zeros((gout_f.shape[0] - half_pad, width), F32)
    gout_f[half_slots : half_slots + half_pad, :] = cot_pair[1].astype(F32)
    gout[...] = gout_f[0:padded, :].astype(BF16)
    up[...] = dot_nt(gout[...], out_weight[...])

    def gate_rows(block):
        rows = rows_at(block)
        value = pz[rows, :]
        logistic = jax.nn.sigmoid(value)
        silu = value * logistic
        half_grad = 0.5 * up[rows, :]
        gate[rows, :] = 0.5 * silu
        zslope[rows, :] = half_grad * logistic * (1.0 + value * (1.0 - logistic))
        up[rows, :] = half_grad * silu

    each_block(gate_rows)

    send_part.wait()

    diagonal = jnp.where(iota((BLOCK, 1024), 0) == (iota((BLOCK, 1024), 1) // state) % BLOCK, 1.0, 0.0)

    def proj_rows(block):
        rows = rows_at(block)
        low = (part[rows, :] + part_in[rows, :]).astype(BF16)
        projb[rows, :] = low
        value = low.astype(F32)
        turned_rows[block] = value.T
        blkm[rows, :] = (dot(low, sel[...]) * diagonal).astype(BF16)

    each_block(proj_rows, 1)

    for r in range(2):
        sig[r] = dot(projb[...], dtw_pad[r])

    def delta_rows(block):
        rows = rows_at(block)
        for r in range(2):
            pre = sig[r, rows, :] + dt_bias[r : r + 1, :]
            small = jnp.exp(-jnp.abs(pre))
            inv = 1.0 / (1.0 + small)
            sig[r, rows, :] = jnp.where(pre >= 0.0, inv, small * inv)
            soft_plus = jnp.maximum(pre, 0.0) + jnp.log1p(small)
            delta[r, rows, :] = soft_plus
            u[r, rows, :] = soft_plus * act[r, rows, :].astype(F32)

    each_block(delta_rows, 1)

    def state_rows(place):
        return pl.ds(pl.multiple_of(place * 16, 16), 16)

    def emit_y(step):
        for r in range(2):
            block = step if r == 0 else blocks - 1 - step
            first_row = block * 256 + (16 if r == 0 else 0)
            held = states[r, pl.ds(pl.multiple_of(first_row, 16), 256), :]
            ys[r, rows_at(block), :] = dot(
                blkm[rows_at(block), 512 * r + 256 : 512 * r + 512], held
            )

    def forward_step(step, carry):
        emit_y(jnp.maximum(step - 1, 0))
        out = []
        for r in range(2):
            held = carry[r]
            block = step if r == 0 else blocks - 1 - step
            base = block * BLOCK
            b_cols = turned_rows[block, 64 * r + rank : 64 * r + rank + state, :]
            for j in range(BLOCK):
                t = j if r == 0 else BLOCK - 1 - j
                decay = jnp.exp2(delta[r, pl.ds(base + t, 1), :] * rates2[r])
                b_wide = jnp.broadcast_to(b_cols[:, t : t + 1], (state, inner_w))
                held = decay * held + u[r, pl.ds(base + t, 1), :] * b_wide
                states[r, state_rows(base + t + (1 if r == 0 else 0)), :] = held.astype(BF16)
            out.append(held)
        return tuple(out)

    zero_state = jnp.zeros((state, inner_w), F32)
    lax.fori_loop(0, blocks, forward_step, (zero_state, zero_state))
    emit_y(blocks - 1)

    def mix_rows(block):
        rows = rows_at(block)
        summed = ys[0, rows, :] + ys[1, rows, :]
        for r in range(2):
            summed = summed + skip_gain[r : r + 1, :] * act[r, rows, :].astype(F32)
        gated[rows, :] = (summed * gate[rows, :]).astype(BF16)
        zgrad[rows, :] = (summed * zslope[rows, :]).astype(BF16)

    each_block(mix_rows)
    terms[0:padded, :] = dot(gated[...], out_weight[...])
    terms_pair[0] = terms[0:half_pad, :]
    terms_pair[1] = terms[half_slots : half_slots + half_pad, :]
    send_terms = remote(terms_pair.at[peer], terms_in, 3)
    send_terms.start()
    out_grad[...] = dot_tn(gated[...], gout[...])
    in_grad[1] = dot_tn(normed[...], zgrad[...])
    npart[...] = dot_nt(zgrad[...], in_weight[1])

    adj_refs, car_refs = (adj_0, adj_1), (car_0, car_1)
    bsum_refs, csum_refs = (bsum_0, bsum_1), (csum_0, csum_1)
    block_mask = diagonal[:, 0:256]
    ones_block = block_mask.astype(BF16)
    ones_rows = jnp.ones((BLOCK, 128), BF16)

    def fold_lanes(value):
        total = value[:, 0:128]
        for at in range(128, inner_w, 128):
            total = total + value[:, at : at + 128]
        return total.astype(BF16)

    def emit_back(step):
        for r in range(2):
            block = blocks - 1 - step if r == 0 else step
            rows = rows_at(block)
            s1[r, rows, :] = dot(blkm[rows, 512 * r : 512 * r + 256], adj_refs[r][...])
            cas[r, rows, :] = dot(ones_block, car_refs[r][...])
            b_sums = dot_nt(ones_rows, bsum_refs[r][...])
            c_sums = dot_nt(ones_rows, csum_refs[r][...])
            pgm[rows, 512 * r : 512 * r + 256] = (b_sums * block_mask).astype(BF16)
            pgm[rows, 512 * r + 256 : 512 * r + 512] = (c_sums * block_mask).astype(BF16)

    def backward_step(step, carry):
        emit_back(jnp.maximum(step - 1, 0))
        out = []
        for r in range(2):
            passed, rate_sum, after = carry[r]
            block = blocks - 1 - step if r == 0 else step
            base = block * BLOCK
            c_cols = turned_rows[block, 64 * r + rank + state : 64 * r + rank + 2 * state, :]
            for j in range(BLOCK):
                t = BLOCK - 1 - j if r == 0 else j
                own = slice(t * 16, t * 16 + 16)
                step_size = delta[r, pl.ds(base + t, 1), :]
                upstream = up[pl.ds(base + t, 1), :]
                decay = jnp.exp2(step_size * rates2[r])
                c_wide = jnp.broadcast_to(c_cols[:, t : t + 1], (state, inner_w))
                adjoint = upstream * c_wide + passed
                passed = decay * adjoint
                adj_refs[r][own, :] = adjoint.astype(BF16)
                before = states[r, state_rows(base + t + (0 if r == 0 else 1)), :].astype(F32)
                carried = passed * before
                car_refs[r][own, :] = (carried * rates[r]).astype(BF16)
                rate_sum = rate_sum + carried * step_size
                bsum_refs[r][own, :] = fold_lanes(adjoint * u[r, pl.ds(base + t, 1), :])
                csum_refs[r][own, :] = fold_lanes(after * upstream)
                after = before
            out.append((passed, rate_sum, after))
        return tuple(out)

    last = states[0, padded * 16 : padded * 16 + 16, :].astype(F32)
    top = states[1, 0:16, :].astype(F32)
    final = lax.fori_loop(
        0,
        blocks,
        backward_step,
        ((zero_state, zero_state, last), (zero_state, zero_state, top)),
    )
    emit_back(blocks - 1)
    for r in range(2):
        alog_grad[r] = final[r][1] * rates[r]

    def soft_rows(block, carry):
        rows = rows_at(block)
        slot = iota((BLOCK, 1), 0) + block * BLOCK
        valid = slot < count
        out = []
        upstream = up[rows, :]
        for r in range(2):
            bias_sum, skip_sum, delta_sum, square_sum = carry[r]
            active = act[r, rows, :].astype(F32)
            step_size = delta[r, rows, :]
            first_sum = s1[r, rows, :]
            pre_grad = (active * first_sum + cas[r, rows, :]) * sig[r, rows, :]
            soft[r, rows, :] = pre_grad.astype(BF16)
            actg[r, rows, :] = first_sum * step_size + skip_gain[r : r + 1, :] * upstream
            kept_step = jnp.where(valid, step_size, 0.0)
            out.append(
                (
                    bias_sum + pre_grad,
                    skip_sum + upstream * active,
                    delta_sum + kept_step,
                    square_sum + kept_step * step_size,
                )
            )
        return tuple(out)

    wide = jnp.zeros((BLOCK, inner_w), F32)
    sums = lax.fori_loop(0, blocks, soft_rows, ((wide,) * 4,) * 2)
    pgrad[...] = (
        dot_nt(pgm[...], sel[...]) + dot_nt(soft[0], dtw_pad[0]) + dot_nt(soft[1], dtw_pad[1])
    )
    send_pgrad = remote(pgrad, pgrad_in, 4)
    send_pgrad.start()
    for r in range(2):
        dtb_grad[r : r + 1, :] = jnp.sum(sums[r][0], axis=0, keepdims=True)
        skip_grad[r : r + 1, :] = jnp.sum(sums[r][1], axis=0, keepdims=True)
        dt_sums[r : r + 1, :] = jnp.sum(sums[r][2], axis=0, keepdims=True)
        dt_sums[2 + r : 3 + r, :] = jnp.sum(sums[r][3], axis=0, keepdims=True)
        low_grad = dot_tn(projb[...], soft[r])
        dtw_grad[r] = low_grad[64 * r : 64 * r + rank, :]

    send_terms.wait()
    gathered_half = jnp.where(
        inner == 0, gathered[0:half_slots, :], gathered[half_slots : 2 * half_slots, :]
    )
    mixer = terms_pair[inner][0:half_slots, :] + terms_in[0:half_slots, :]
    output[...] = jnp.where(cot_rows < count, gathered_half + mixer, 0.0).astype(BF16)

    send_pgrad.wait()
    pgb[...] = (pgrad[...] + pgrad_in[...]).astype(BF16)
    for r in range(2):
        actg[r] = actg[r] + dot_nt(pgb[...], xw_cat[r])

    def back_rows(block):
        rows = rows_at(block)
        inside = pl.ds(pl.multiple_of(block * BLOCK, BLOCK) + 8, BLOCK)
        for r in range(2):
            cgrad[r, inside, :] = actg[r, rows, :] * slope[r, rows, :]

    each_block(back_rows)

    def conv_back_rows(block, carry):
        base = pl.multiple_of(block * BLOCK, BLOCK)
        window = px[pl.ds(base, BLOCK + 16), :]
        total = jnp.zeros((BLOCK, inner_w), F32)
        out = []
        for r in range(2):
            grads = cgrad[r, pl.ds(base, BLOCK + 16), :]
            here = grads[8 : 8 + BLOCK, :]
            for k in range(4):
                shift = k - 3 if r == 0 else 3 - k
                total = total + taps[r, k : k + 1, :] * grads[8 - shift : 8 - shift + BLOCK, :]
                out.append(carry[5 * r + k] + here * window[8 + shift : 8 + shift + BLOCK, :])
            out.append(carry[5 * r + 4] + here)
        xgrad[rows_at(block), :] = total.astype(BF16)
        return tuple(out)

    conv_sums = lax.fori_loop(0, blocks, conv_back_rows, (wide,) * 10)
    npart[...] = npart[...] + dot_nt(xgrad[...], in_weight[0])
    send_npart = remote(npart, npart_in, 5)
    send_npart.start()
    for r in range(2):
        for k in range(4):
            conv_w_grad[r, k : k + 1, :] = jnp.sum(conv_sums[5 * r + k], axis=0, keepdims=True)
        conv_b_grad[r : r + 1, :] = jnp.sum(conv_sums[5 * r + 4], axis=0, keepdims=True)
        wide_grad = dot_tn(act[r], pgb[...])
        xw_grad[r] = wide_grad[:, 64 * r : 64 * r + rank + 2 * state]
    in_grad[0] = dot_tn(normed[...], xgrad[...])

    send_npart.wait()

    def slot_rows(block, carry):
        rows = rows_at(block)
        whole = npart[rows, :] + npart_in[rows, :]
        held = gathered[rows, :]
        scale = inverse[rows, :]
        by_gain = whole * held * scale
        scaled = whole * gain
        row_dot = jnp.sum(scaled * held, axis=1, keepdims=True)
        factor = scale * scale * scale * row_dot / width
        grad = scale * scaled - held * factor + gout_f[rows, :]
        slot = iota((BLOCK, 1), 0) + block * BLOCK
        sgrad[rows, :] = jnp.where(slot < count, grad, 0.0).astype(BF16)
        return carry + by_gain

    gain_sum = lax.fori_loop(0, blocks, slot_rows, wide)
    gain_grad[...] = jnp.sum(gain_sum, axis=0, keepdims=True)

    slot_lane = iota((1, slots), 1)
    places = jnp.where(slot_lane < count, kept_row - first, -1.0)
    spread = 112

    def scatter_rows(step, carry):
        base = pl.multiple_of(step * spread, 16)
        row = (iota((spread, slots), 0) + step * spread).astype(F32)
        chosen = jnp.where(row == places, 1.0, 0.0).astype(BF16)
        hidden_grad[pl.ds(base, spread), :] = dot(chosen, sgrad[0:slots, :]).astype(BF16)
        return carry

    lax.fori_loop(0, half_full // spread, scatter_rows, 0)


def per_device(
    hidden,
    kept,
    counts,
    norm_gain,
    in_weight,
    conv_weight,
    conv_bias,
    x_weight,
    dt_weight,
    dt_bias,
    a_log,
    skip_gain,
    out_weight,
    cotangent,
):
    half_full, width = hidden.shape[1:]
    slots = kept.shape[1]
    half_slots = cotangent.shape[1]
    padded = round_up(slots, BLOCK)
    half_pad = round_up(half_slots, BLOCK)
    inner_w = in_weight.shape[2]
    rank = dt_weight.shape[1]
    state = a_log.shape[1]
    xwidth = x_weight.shape[2]
    sizes = (half_full, width, slots, padded, half_slots, half_pad, inner_w, rank, state)
    inner_index = lax.axis_index("inner")
    inner_count = lax.axis_size("inner")

    def shape(*dims, kind=F32):
        return jax.ShapeDtypeStruct(dims, kind)

    outs = [
        shape(half_slots, width, kind=BF16),
        shape(half_full, width, kind=BF16),
        shape(1, width),
        shape(2, width, inner_w),
        shape(2, 4, inner_w),
        shape(2, inner_w),
        shape(2, inner_w, xwidth),
        shape(2, rank, inner_w),
        shape(2, inner_w),
        shape(2, state, inner_w),
        shape(2, inner_w),
        shape(inner_w, width),
        shape(4, inner_w),
    ]
    vm = pltpu.VMEM
    scratch = [
        vm((padded, width), BF16),
        vm((padded, width), BF16),
        vm((2, half_pad, width), BF16),
        vm((round_up(half_slots + half_pad, BLOCK) + 16, width), F32),
        vm((padded, width), BF16),
        vm((padded, width), F32),
        vm((padded, 1), F32),
        vm((padded, width), BF16),
        vm((padded + 16, inner_w), F32),
        vm((padded, inner_w), F32),
        vm((2, padded, inner_w), F32),
        vm((2, padded, inner_w), BF16),
        vm((2, inner_w, 128), BF16),
        vm((2, 128, inner_w), BF16),
        vm((2, state, inner_w), F32),
        vm((2, state, inner_w), F32),
        vm((padded, 128), F32),
        vm((padded, 128), F32),
        vm((padded, 128), F32),
        vm((padded, 128), BF16),
        vm((2, padded, inner_w), F32),
        vm((2, padded, inner_w), F32),
        vm((2, padded, inner_w), F32),
        vm((padded, inner_w), F32),
        vm((padded, inner_w), F32),
        vm((padded, inner_w), F32),
        vm((padded, inner_w), BF16),
        vm((padded, inner_w), BF16),
        vm((round_up(half_slots + half_pad, BLOCK), width), F32),
        vm((2, half_pad, width), F32),
        vm((half_pad, width), F32),
        vm((padded, 1024), BF16),
        vm((padded // BLOCK, 128, BLOCK), F32),
        vm((128, 1024), BF16),
        vm((2, padded * 16 + 16, inner_w), BF16),
        vm((2, padded, inner_w), F32),
        vm((256, inner_w), BF16),
        vm((256, inner_w), BF16),
        vm((256, inner_w), BF16),
        vm((256, inner_w), BF16),
        vm((256, 128), BF16),
        vm((256, 128), BF16),
        vm((256, 128), BF16),
        vm((256, 128), BF16),
        vm((2, padded, inner_w), F32),
        vm((2, padded, inner_w), F32),
        vm((padded, 1024), BF16),
        vm((2, padded, inner_w), BF16),
        vm((2, padded, inner_w), F32),
        vm((padded, 128), F32),
        vm((padded, 128), F32),
        vm((padded, 128), BF16),
        vm((2, padded + 16, inner_w), F32),
        vm((padded, inner_w), BF16),
        vm((padded, width), F32),
        vm((padded, width), BF16),
        vm((padded, width), F32),
        vm((padded, width), BF16),
        pltpu.SemaphoreType.DMA((6,)),
        pltpu.SemaphoreType.DMA((6,)),
    ]
    in_vmem = pl.BlockSpec(memory_space=pltpu.VMEM)
    in_smem = pl.BlockSpec(memory_space=pltpu.SMEM)
    in_specs = [in_vmem, in_vmem, in_smem] + [in_vmem] * 11
    (
        output,
        hidden_grad,
        gain_whole,
        in_grad,
        conv_w_grad,
        conv_b_grad,
        xw_grad,
        dtw_grad,
        dtb_grad,
        alog_grad,
        skip_grad,
        out_grad,
        dt_sums,
    ) = pl.pallas_call(
        functools.partial(block_kernel, sizes),
        out_shape=outs,
        in_specs=in_specs,
        out_specs=[in_vmem] * len(outs),
        scratch_shapes=scratch,
        compiler_params=pltpu.CompilerParams(
            collective_id=0, has_side_effects=True, vmem_limit_bytes=63 * 2**20
        ),
    )(
        hidden[0],
        kept,
        counts,
        norm_gain[None],
        in_weight,
        conv_weight,
        conv_bias,
        x_weight,
        dt_weight,
        dt_bias,
        a_log,
        skip_gain,
        out_weight,
        cotangent[0],
    )
    gain_part = width // inner_count
    gain_grad = lax.dynamic_slice_in_dim(gain_whole[0], inner_index * gain_part, gain_part, 0)
    kept_total = jnp.sum(counts).astype(F32)
    (
        gain_grad,
        in_grad,
        conv_w_grad,
        conv_b_grad,
        xw_grad,
        dtw_grad,
        dtb_grad,
        alog_grad,
        skip_grad,
        out_grad,
        dt_sums,
        kept_total,
    ) = lax.psum(
        (
            gain_grad,
            in_grad,
            conv_w_grad,
            conv_b_grad,
            xw_grad,
            dtw_grad,
            dtb_grad,
            alog_grad,
            skip_grad,
            out_grad,
            dt_sums,
            kept_total,
        ),
        "rows",
    )
    dt_mean = dt_sums[0:2] / kept_total
    dt_var = dt_sums[2:4] / kept_total - dt_mean * dt_mean
    return (
        output[None],
        hidden_grad[None],
        gain_grad,
        in_grad,
        conv_w_grad,
        conv_b_grad,
        xw_grad,
        dtw_grad,
        dtb_grad,
        alog_grad,
        skip_grad,
        out_grad,
        dt_mean,
        dt_var,
    )


def solution(mesh):
    in_specs = (
        P("rows", "inner", None),
        P("rows", None),
        P("rows"),
        P(),
        P(None, None, "inner"),
        P(None, None, "inner"),
        P(None, "inner"),
        P(None, "inner", None),
        P(None, None, "inner"),
        P(None, "inner"),
        P(None, None, "inner"),
        P(None, "inner"),
        P("inner", None),
        P("rows", "inner", None),
    )
    out_specs = (
        P("rows", "inner", None),
        P("rows", "inner", None),
        P("inner"),
        P(None, None, "inner"),
        P(None, None, "inner"),
        P(None, "inner"),
        P(None, "inner", None),
        P(None, None, "inner"),
        P(None, "inner"),
        P(None, None, "inner"),
        P(None, "inner"),
        P("inner", None),
        P(None, "inner"),
        P(None, "inner"),
    )
    return jax.shard_map(
        per_device, mesh=mesh, in_specs=in_specs, out_specs=out_specs, check_vma=False
    )
```

profile of v0, /device:TPU:0, one launch (start us, length us, event | category | flops | bytes accessed | tf_op | source)
XLA Modules:
  0.0 215.4 jit_solution(15602521203425104235)
XLA Ops:
  7.2 0.0 all-reduce.5.cloned.1.call-start
  7.9 1.7 copy.28.x_weight
  9.6 1.2 broadcast_in_dim.9.norm_gain
  10.8 56.8 %shard_map.245 = (bf16[196,384]{1,0:T(8,128)(2,1)}, bf16[784,384]{1,0:T(8,128)(2,1)}, f32[1,384]{1,0:T(1,128)}, f32[2,384,384]{2,1,0:T(8,128)}, f32[2,4,384]{2,1...) custom-call(bf16[784,384]{1,0:T(8,128)(2,1)} %bitcast.6, ...), custom_call_target="tpu_custom_call" | custom-call | tf_op jit(solution)/shard_map/pallas_call | solution.py:662
  67.7 0.0 copy-start.11
  67.7 0.0 copy-start.5
  67.7 0.0 copy-start.6
  67.7 0.0 copy-start.7
  67.7 0.0 copy-start.8
  67.7 0.0 copy-start.9
  67.7 0.0 copy-start.10
  67.7 0.0 copy-start.3
  67.7 0.0 copy-start.1
  67.7 0.0 all-reduce.5.cloned.1.call-update
  67.8 0.6 copy-done.11
  68.3 0.1 constant_dynamic-slice_fusion
  68.4 0.1 copy-done.5
  68.5 0.0 copy-done.6
  68.5 0.0 copy-done.7
  68.5 0.0 copy-done.8
  68.5 0.0 copy-done.9
  68.5 0.0 copy-done.10
  68.5 82.3 %all-reduce.6 = (f32[192]{0:T(256)}, f32[2,4,384]{2,1,0:T(4,128)}, f32[2,384]{1,0:T(2,128)}, f32[2,384]{1,0:T(2,128)}, f32[2,16,384]{2,1,0:T(8,128)}, /*index=5*...) all-reduce(f32[192]{0:T(256)S(1)} %bitcast.10, ...), channel_id=1, replica_groups=mesh['rows'=16,'inner'=2] {'rows'}, use_global_device_ids=true, to_apply=%region_0.0 | all-reduce | flops 19393 | bytes 155144 | tf_op jit(solution)/shard_map/psum | solution.py:703
  150.8 1.2 divide_subtract_fusion
  152.1 50.6 %all-reduce.5.cloned.1.call-done = (f32[2,384,384]{2,1,0:T(8,128)}, f32[2,384,56]{2,1,0:T(8,128)}, f32[2,24,384]{2,1,0:T(8,128)}, f32[384,384]{1,0:T(8,128)}) async-done(((f32[2,384,384]{2,1,0:T(8,128)}, f32[2,384,56]{2,1,0:T(8,128)}, f32[2,24,384]{2,1,0:T(8,128)}, f32[384,384]{1,0:T(8,128)}), (f32[2,384,384]{2,1,0:T(8,128)}, f32[2,384,56]{2,1,0:T(8,128)}, f32[2,24,384]{2,1,0:T(8,128)}, ...) | async-done | bytes 2015248 | tf_op jit(solution)/shard_map/psum | solution.py:703
  202.7 0.0 copy-start
  202.7 1.9 copy.29
  204.6 0.0 copy-done.3
  204.6 0.7 copy.53
  205.3 0.0 copy-done.1
  205.3 0.8 copy.54
  206.1 0.0 copy-done
  206.1 0.0 copy-start.4
  206.1 0.0 copy-start.2
  206.1 1.0 copy.55
  207.1 0.0 copy-done.4
  207.1 0.6 copy.56
  207.8 0.0 copy-done.2
  207.8 0.8 copy.57
Async XLA Ops:
  7.2 195.5 %all-reduce.5.cloned.1.call-start = ((), (), s32[]{:S(2)}) async-start(), calls=%async_computation | async-start | bytes 4472832 | tf_op jit(solution)/shard_map/psum | solution.py:703
  67.7 0.7 copy-start.11
  67.7 0.8 copy-start.5
  67.7 0.8 copy-start.6
  67.7 0.8 copy-start.7
  67.7 0.8 copy-start.8
  67.7 0.8 copy-start.9
  67.7 0.8 copy-start.10
  67.7 136.9 %copy-start.3 = (bf16[196,384]{1,0:T(8,128)(2,1)S(1)}, bf16[196,384]{1,0:T(8,128)(2,1)}, u32[]{:S(2)}) copy-start(bf16[196,384]{1,0:T(8,128)(2,1)} %get-tuple-element.27) | copy-start | bytes 451588
  67.7 137.6 %copy-start.1 = (bf16[784,384]{1,0:T(8,128)(2,1)S(1)}, bf16[784,384]{1,0:T(8,128)(2,1)}, u32[]{:S(2)}) copy-start(bf16[784,384]{1,0:T(8,128)(2,1)} %get-tuple-element.28) | copy-start | bytes 1806340
  202.7 3.4 %copy-start = (f32[2,384,384]{2,1,0:T(8,128)S(1)}, f32[2,384,384]{2,1,0:T(8,128)}, u32[]{:S(2)}) copy-start(f32[2,384,384]{2,1,0:T(8,128)} %get-tuple-element.85) | copy-start | bytes 3538948
  206.1 1.0 copy-start.4
  206.1 1.7 copy-start.2
Sparse Core Ops, SparseCore 0:
  67.9 134.7 all-reduce.4
where the time goes:
time: 216 us; the launch traced here: 215 us
  blocking collectives  82.3 us (38%)
  Pallas kernels  56.8 us (26%)
  waiting for transfers between devices  50.7 us (23%)
  between operations  14.8 us (7%)
  local copies, waits for them, and re-layouts  9.53 us (4%)
    psum x1, blocking collectives, per_device(): lax.psum((gain_grad, in_grad, conv_w_grad, conv_b_grad, xw_grad, dtw_grad...  82.3 us
    pallas_call x1, Pallas kernels, per_device(): pl.pallas_call(functools.partial(block_kernel, sizes), out_shape=outs, in...  56.8 us
    psum x1, waiting for transfers between devices, per_device(): lax.psum((gain_grad, in_grad, conv_w_grad, conv_b_grad, xw_grad, dtw_grad...  50.6 us
    unnamed x31, local copies, waits for them, and re-layouts  8.21 us
  transfers between devices with their start and end apart: 1, of which 1 were waited for; matrix products, arithmetic and copies ran while one was open for 1% of the time, Pallas kernels for 0%

commit v1 on v0

--- a/solution.py
+++ b/solution.py
@@ -33,6 +33,101 @@
 
 def round_up(value, unit):
     return (value + unit - 1) // unit * unit
+
+
+def chunk_tiles(total, devices):
+    first = -(-2 * total // (3 * devices))
+    return first, max(1, -(-(total - first * devices) // devices))
+
+
+def tile_at(pair, tile):
+    ref = pair[0]
+    capacity = ref.shape[0] * ref.shape[1] * ref.shape[2] // BLOCK
+    if tile >= capacity:
+        tile, ref = tile - capacity, pair[1]
+    each = ref.shape[2] // BLOCK
+    chunk, place = tile // each, tile % each
+    outer, middle = chunk // ref.shape[1], chunk % ref.shape[1]
+    return ref, (outer, middle, slice(place * BLOCK, place * BLOCK + BLOCK), slice(None))
+
+
+class Reducer:
+    def __init__(self, a, b, sems, near, far, my_near, my_far, near_peer, far_peer):
+        self.ways = [
+            (a, (near, my_near, near_peer), (far, my_far, far_peer)),
+            (b, (far, my_far, far_peer), (near, my_near, near_peer)),
+        ]
+        self.sems = sems
+        self.copies = []
+
+    def put(self, first, value):
+        columns = value.shape[1] // 128
+        pair = (self.ways[0][0][0], self.ways[1][0][0])
+        for tile in range(value.shape[0] // BLOCK):
+            for lane in range(columns):
+                ref, at = tile_at(pair, first + tile * columns + lane)
+                part = value[tile * BLOCK : tile * BLOCK + BLOCK, lane * 128 : lane * 128 + 128]
+                ref[at] = part.astype(BF16)
+
+    def send(self, phase, make):
+        self.copies = []
+        place = 0
+        for refs, one, two in self.ways:
+            number, mine, peer_of = one if phase in (0, 3) else two
+            for offset in range(1, number):
+                source, target = make(refs, one, two, lax.rem(mine + offset, number))
+                copy = pltpu.make_async_remote_copy(
+                    src_ref=source,
+                    dst_ref=target,
+                    send_sem=self.sems.at[phase, 0, place],
+                    recv_sem=self.sems.at[phase, 1, place],
+                    device_id={"rows": peer_of(offset)},
+                    device_id_type=MESH,
+                )
+                copy.start()
+                self.copies.append(copy)
+                place += 1
+
+    def wait(self):
+        for copy in self.copies:
+            copy.wait()
+
+    def first(self):
+        self.send(0, lambda refs, one, two, other: (refs[0].at[other], refs[1].at[one[1]]))
+
+    def second(self):
+        self.wait()
+        for refs, one, two in self.ways:
+            number, mine, _ = one
+            for part in range(two[0]):
+                held = refs[0][mine, part].astype(F32)
+                for offset in range(1, number):
+                    held = held + refs[1][lax.rem(mine + offset, number), part].astype(F32)
+                refs[2][part] = held.astype(BF16)
+        self.send(1, lambda refs, one, two, other: (refs[2].at[other], refs[3].at[two[1]]))
+
+    def third(self):
+        self.wait()
+        for refs, one, two in self.ways:
+            number, mine, _ = two
+            held = refs[2][mine].astype(F32)
+            for offset in range(1, number):
+                held = held + refs[3][lax.rem(mine + offset, number)].astype(F32)
+            refs[4][one[1], mine] = held.astype(BF16)
+        self.send(
+            2,
+            lambda refs, one, two, other: (
+                refs[4].at[one[1], two[1]],
+                refs[4].at[one[1], two[1]],
+            ),
+        )
+
+    def fourth(self):
+        self.wait()
+        self.send(3, lambda refs, one, two, other: (refs[4].at[one[1]], refs[4].at[one[1]]))
+
+    def finish(self):
+        self.wait()
 
 
 def block_kernel(
@@ -53,17 +148,11 @@
     cotangent,
     output,
     hidden_grad,
-    gain_grad,
-    in_grad,
-    conv_w_grad,
-    conv_b_grad,
-    xw_grad,
-    dtw_grad,
-    dtb_grad,
-    alog_grad,
-    skip_grad,
-    out_grad,
-    dt_sums,
+    early_a_out,
+    early_b_out,
+    late_a_out,
+    late_b_out,
+    tiny_out,
     picked,
     picked_in,
     cot_pair,
@@ -122,10 +211,35 @@
     npart_b,
     npart_in,
     sgrad,
+    chosen,
+    spread_rows,
+    early_a,
+    early_a1,
+    early_am,
+    early_a2,
+    early_b,
+    early_b1,
+    early_bm,
+    early_b2,
+    late_a,
+    late_a1,
+    late_am,
+    late_a2,
+    late_b,
+    late_b1,
+    late_bm,
+    late_b2,
+    tiny,
+    tiny_low,
+    tiny_mid,
+    tiny_high,
     send_sem,
     recv_sem,
+    early_sems,
+    late_sems,
+    tiny_sems,
 ):
-    half_full, width, slots, padded, half_slots, half_pad, inner_w, rank, state = sizes
+    half_full, width, slots, padded, half_slots, half_pad, inner_w, rank, state, near, far = sizes
     blocks = padded // BLOCK
     inner = lax.axis_index("inner")
     peer = 1 - inner
@@ -150,8 +264,36 @@
 
         lax.fori_loop(0, blocks, step, 0, unroll=unroll)
 
+    row = lax.axis_index("rows")
+    my_near, my_far = lax.rem(row, near), row // near
+
+    def near_peer(offset):
+        return my_far * near + lax.rem(my_near + offset, near)
+
+    def far_peer(offset):
+        return lax.rem(my_far + offset, far) * near + my_near
+
     barrier = pltpu.get_barrier_semaphore()
     pl.semaphore_signal(barrier, inc=1, device_id={"inner": peer}, device_id_type=MESH)
+    for offset in range(1, near):
+        pl.semaphore_signal(
+            barrier, inc=1, device_id={"rows": near_peer(offset)}, device_id_type=MESH
+        )
+    for offset in range(1, far):
+        pl.semaphore_signal(
+            barrier, inc=1, device_id={"rows": far_peer(offset)}, device_id_type=MESH
+        )
+
+    early = Reducer(
+        (early_a, early_a1, early_am, early_a2, early_a_out),
+        (early_b, early_b1, early_bm, early_b2, early_b_out),
+        early_sems, near, far, my_near, my_far, near_peer, far_peer,
+    )
+    late = Reducer(
+        (late_a, late_a1, late_am, late_a2, late_a_out),
+        (late_b, late_b1, late_bm, late_b2, late_b_out),
+        late_sems, near, far, my_near, my_far, near_peer, far_peer,
+    )
 
     count = counts[0]
     kept_row = kept[...].astype(F32)
@@ -170,27 +312,25 @@
         slot = iota((BLOCK, 1), 0) + block * BLOCK
         place = jnp.where(slot < count, place, -1.0)
         column = iota((BLOCK, half_full), 1).astype(F32)
-        chosen = jnp.where(place == column, 1.0, 0.0).astype(BF16)
-        picked[rows_at(block), :] = dot(chosen, hidden[...]).astype(BF16)
-
-    each_block(pick_rows, 1)
-    pl.semaphore_wait(barrier, 1)
+        chosen[rows_at(block), :] = jnp.where(place == column, 1.0, 0.0).astype(BF16)
+
+    each_block(pick_rows)
+    picked[...] = dot(chosen[...], hidden[...]).astype(BF16)
+    pl.semaphore_wait(barrier, near + far - 1)
     send_pick = remote(picked, picked_in, 0)
     send_pick.start()
     send_cot = remote(cot_pair.at[inner], cot_pair.at[inner], 1)
     send_cot.start()
 
-    pad_lane = jnp.zeros((inner_w, 64 - rank - 2 * state), F32)
-    for r in range(2):
-        mine = jnp.concatenate([x_weight[r].astype(F32), pad_lane], 1)
-        other = jnp.zeros((inner_w, 64), F32)
-        both = [mine, other] if r == 0 else [other, mine]
-        xw_cat[r] = jnp.concatenate(both, 1).astype(BF16)
-        low = dt_weight[r].astype(F32)
-        parts = [low, jnp.zeros((128 - 64 * r - rank, inner_w), F32)]
+    def at_rows(value, r):
+        parts = [value, jnp.zeros((128 - 64 * r - value.shape[0], inner_w), F32)]
         if r:
             parts = [jnp.zeros((64 * r, inner_w), F32)] + parts
-        dtw_pad[r] = jnp.concatenate(parts, 0).astype(BF16)
+        return jnp.concatenate(parts, 0).astype(BF16)
+
+    for r in range(2):
+        xw_cat[r] = at_rows(x_weight[r].astype(F32), r)
+        dtw_pad[r] = at_rows(dt_weight[r].astype(F32), r)
         rate = -jnp.exp(a_log[r])
         rates[r] = rate
         rates2[r] = rate * LOG2E
@@ -212,7 +352,7 @@
     states[1, padded * 16 : padded * 16 + 16, :] = jnp.zeros((16, inner_w), BF16)
 
     send_pick.wait()
-    gain = norm_gain[...]
+    gain = norm_gain[...].reshape(1, width)
 
     def norm_rows(block):
         rows = rows_at(block)
@@ -243,8 +383,8 @@
             act[r, rows, :] = (total * logistic * valid).astype(BF16)
             slope[r, rows, :] = logistic * (1.0 + total * (1.0 - logistic)) * valid
 
-    each_block(conv_rows, 1)
-    part[...] = dot(act[0], xw_cat[0]) + dot(act[1], xw_cat[1])
+    each_block(conv_rows)
+    part[...] = dot_nt(act[0], xw_cat[0]) + dot_nt(act[1], xw_cat[1])
     send_part = remote(part, part_in, 2)
     send_part.start()
 
@@ -277,9 +417,15 @@
         projb[rows, :] = low
         value = low.astype(F32)
         turned_rows[block] = value.T
-        blkm[rows, :] = (dot(low, sel[...]) * diagonal).astype(BF16)
-
-    each_block(proj_rows, 1)
+
+    each_block(proj_rows)
+    spread_rows[...] = dot(projb[...], sel[...])
+
+    def mask_rows(block):
+        rows = rows_at(block)
+        blkm[rows, :] = (spread_rows[rows, :] * diagonal).astype(BF16)
+
+    each_block(mask_rows)
 
     for r in range(2):
         sig[r] = dot(projb[...], dtw_pad[r])
@@ -295,7 +441,7 @@
             delta[r, rows, :] = soft_plus
             u[r, rows, :] = soft_plus * act[r, rows, :].astype(F32)
 
-    each_block(delta_rows, 1)
+    each_block(delta_rows)
 
     def state_rows(place):
         return pl.ds(pl.multiple_of(place * 16, 16), 16)
@@ -344,8 +490,9 @@
     terms_pair[1] = terms[half_slots : half_slots + half_pad, :]
     send_terms = remote(terms_pair.at[peer], terms_in, 3)
     send_terms.start()
-    out_grad[...] = dot_tn(gated[...], gout[...])
-    in_grad[1] = dot_tn(normed[...], zgrad[...])
+    early.put(0, dot_tn(gated[...], gout[...]))
+    early.put(inner_w // BLOCK * (width // 128), dot_tn(normed[...], zgrad[...]))
+    early.first()
     npart[...] = dot_nt(zgrad[...], in_weight[1])
 
     adj_refs, car_refs = (adj_0, adj_1), (car_0, car_1)
@@ -401,15 +548,21 @@
 
     last = states[0, padded * 16 : padded * 16 + 16, :].astype(F32)
     top = states[1, 0:16, :].astype(F32)
-    final = lax.fori_loop(
-        0,
-        blocks,
-        backward_step,
-        ((zero_state, zero_state, last), (zero_state, zero_state, top)),
-    )
+    cuts = [0, blocks * 2 // 5, blocks * 7 // 10, blocks]
+    final = ((zero_state, zero_state, last), (zero_state, zero_state, top))
+    final = lax.fori_loop(cuts[0], cuts[1], backward_step, final)
+    early.second()
+    final = lax.fori_loop(cuts[1], cuts[2], backward_step, final)
+    early.third()
+    final = lax.fori_loop(cuts[2], cuts[3], backward_step, final)
     emit_back(blocks - 1)
-    for r in range(2):
-        alog_grad[r] = final[r][1] * rates[r]
+    early.fourth()
+    wide_tiles = inner_w // 128
+    at_xw = width // BLOCK * wide_tiles
+    at_dtw = at_xw + 2 * (rank + 2 * state) // BLOCK * wide_tiles
+    at_alog = at_dtw + 2 * rank // BLOCK * wide_tiles
+    at_small = at_alog + 2 * state // BLOCK * wide_tiles
+    late.put(at_alog, jnp.concatenate([final[r][1] * rates[r] for r in range(2)], 0))
 
     def soft_rows(block, carry):
         rows = rows_at(block)
@@ -443,13 +596,17 @@
     )
     send_pgrad = remote(pgrad, pgrad_in, 4)
     send_pgrad.start()
+    def total(value):
+        return jnp.sum(value, axis=0, keepdims=True)
+
+    low_grads = [
+        dot_tn(projb[...], soft[r])[64 * r : 64 * r + rank, :] for r in range(2)
+    ]
+    late.put(at_dtw, jnp.concatenate(low_grads, 0))
     for r in range(2):
-        dtb_grad[r : r + 1, :] = jnp.sum(sums[r][0], axis=0, keepdims=True)
-        skip_grad[r : r + 1, :] = jnp.sum(sums[r][1], axis=0, keepdims=True)
-        dt_sums[r : r + 1, :] = jnp.sum(sums[r][2], axis=0, keepdims=True)
-        dt_sums[2 + r : 3 + r, :] = jnp.sum(sums[r][3], axis=0, keepdims=True)
-        low_grad = dot_tn(projb[...], soft[r])
-        dtw_grad[r] = low_grad[64 * r : 64 * r + rank, :]
+        tiny[r : r + 1, :] = total(sums[r][2])
+        tiny[2 + r : 3 + r, :] = total(sums[r][3])
+    tiny[5:8, :] = jnp.full((3, inner_w), count.astype(F32))
 
     send_terms.wait()
     gathered_half = jnp.where(
@@ -460,8 +617,11 @@
 
     send_pgrad.wait()
     pgb[...] = (pgrad[...] + pgrad_in[...]).astype(BF16)
+    xwidth = rank + 2 * state
+    xw_grads = [dot_tn(pgb[...], act[r])[64 * r : 64 * r + xwidth, :] for r in range(2)]
+    late.put(at_xw, jnp.concatenate(xw_grads, 0))
     for r in range(2):
-        actg[r] = actg[r] + dot_nt(pgb[...], xw_cat[r])
+        actg[r] = actg[r] + dot(pgb[...], xw_cat[r])
 
     def back_rows(block):
         rows = rows_at(block)
@@ -488,16 +648,16 @@
         return tuple(out)
 
     conv_sums = lax.fori_loop(0, blocks, conv_back_rows, (wide,) * 10)
+    late.put(0, dot_tn(normed[...], xgrad[...]))
+    small = [total(conv_sums[5 * r + k]) for r in range(2) for k in range(4)]
+    small += [total(conv_sums[5 * r + 4]) for r in range(2)]
+    small += [total(sums[r][i]) for i in range(2) for r in range(2)]
+    small += [jnp.zeros((BLOCK - len(small), inner_w), F32)]
+    late.put(at_small, jnp.concatenate(small, 0))
+    late.first()
     npart[...] = npart[...] + dot_nt(xgrad[...], in_weight[0])
     send_npart = remote(npart, npart_in, 5)
     send_npart.start()
-    for r in range(2):
-        for k in range(4):
-            conv_w_grad[r, k : k + 1, :] = jnp.sum(conv_sums[5 * r + k], axis=0, keepdims=True)
-        conv_b_grad[r : r + 1, :] = jnp.sum(conv_sums[5 * r + 4], axis=0, keepdims=True)
-        wide_grad = dot_tn(act[r], pgb[...])
-        xw_grad[r] = wide_grad[:, 64 * r : 64 * r + rank + 2 * state]
-    in_grad[0] = dot_tn(normed[...], xgrad[...])
 
     send_npart.wait()
 
@@ -515,8 +675,27 @@
         sgrad[rows, :] = jnp.where(slot < count, grad, 0.0).astype(BF16)
         return carry + by_gain
 
-    gain_sum = lax.fori_loop(0, blocks, slot_rows, wide)
-    gain_grad[...] = jnp.sum(gain_sum, axis=0, keepdims=True)
+    gain_sum = lax.fori_loop(0, blocks, slot_rows, wide, unroll=5)
+    tiny[4:5, :] = total(gain_sum)
+
+    def tiny_sends(source, target, peer_of, mine, number, base):
+        copies = []
+        for offset in range(1, number):
+            copies.append(
+                pltpu.make_async_remote_copy(
+                    src_ref=source,
+                    dst_ref=target.at[mine],
+                    send_sem=tiny_sems.at[0, base + offset - 1],
+                    recv_sem=tiny_sems.at[1, base + offset - 1],
+                    device_id={"rows": peer_of(offset)},
+                    device_id_type=MESH,
+                )
+            )
+            copies[-1].start()
+        return copies
+
+    copies = tiny_sends(tiny, tiny_low, near_peer, my_near, near, 0)
+    late.second()
 
     slot_lane = iota((1, slots), 1)
     places = jnp.where(slot_lane < count, kept_row - first, -1.0)
@@ -530,6 +709,97 @@
         return carry
 
     lax.fori_loop(0, half_full // spread, scatter_rows, 0)
+    for copy in copies:
+        copy.wait()
+    held = tiny[...]
+    for offset in range(1, near):
+        held = held + tiny_low[lax.rem(my_near + offset, near)]
+    tiny_mid[...] = held
+    copies = tiny_sends(tiny_mid, tiny_high, far_peer, my_far, far, near - 1)
+    late.third()
+    for copy in copies:
+        copy.wait()
+    held = tiny_mid[...]
+    for offset in range(1, far):
+        held = held + tiny_high[lax.rem(my_far + offset, far)]
+    tiny_out[...] = held
+    late.fourth()
+    early.finish()
+    late.finish()
+
+
+def finish_kernel(
+    tiles,
+    early_a,
+    early_b,
+    late_a,
+    late_b,
+    tiny,
+    output_in,
+    hidden_in,
+    inner_ref,
+    output,
+    hidden_grad,
+    gain_grad,
+    in_grad,
+    conv_w_grad,
+    conv_b_grad,
+    xw_grad,
+    dtw_grad,
+    dtb_grad,
+    alog_grad,
+    skip_grad,
+    out_grad,
+    dt_mean,
+    dt_var,
+):
+    rank, state = dtw_grad.shape[1], alog_grad.shape[1]
+    xwidth = rank + 2 * state
+    width, inner_w = in_grad.shape[1:]
+    wide_tiles = inner_w // 128
+
+    def take(pair, first, rows, columns):
+        parts = []
+        for tile in range(rows // BLOCK):
+            line = []
+            for lane in range(columns // 128):
+                ref, at = tile_at(pair, first + tile * (columns // 128) + lane)
+                line.append(ref[at])
+            parts.append(jnp.concatenate(line, 1))
+        return jnp.concatenate(parts, 0).astype(F32)
+
+    early, late = (early_a, early_b), (late_a, late_b)
+    out_grad[...] = take(early, 0, inner_w, width)
+    in_grad[1] = take(early, inner_w // BLOCK * (width // 128), width, inner_w)
+    in_grad[0] = take(late, 0, width, inner_w)
+    at = width // BLOCK * wide_tiles
+    both = take(late, at, 2 * xwidth, inner_w)
+    for r in range(2):
+        xw_grad[r] = both[r * xwidth : (r + 1) * xwidth, :]
+    at += 2 * xwidth // BLOCK * wide_tiles
+    both = take(late, at, 2 * rank, inner_w)
+    for r in range(2):
+        dtw_grad[r] = both[r * rank : (r + 1) * rank, :]
+    at += 2 * rank // BLOCK * wide_tiles
+    both = take(late, at, 2 * state, inner_w)
+    for r in range(2):
+        alog_grad[r] = both[r * state : (r + 1) * state, :]
+    at += 2 * state // BLOCK * wide_tiles
+    small = take(late, at, BLOCK, inner_w)
+    for r in range(2):
+        conv_w_grad[r] = small[4 * r : 4 * r + 4, :]
+    conv_b_grad[...] = small[8:10, :]
+    dtb_grad[...] = small[10:12, :]
+    skip_grad[...] = small[12:14, :]
+    sums = tiny[...]
+    mean = sums[0:2, :] / sums[5:6, :]
+    dt_mean[...] = mean
+    dt_var[...] = sums[2:4, :] / sums[5:6, :] - mean * mean
+    part = width // 2
+    gain = jnp.where(inner_ref[0] == 0, sums[4:5, 0:part], sums[4:5, part:width])
+    gain_grad[...] = gain.reshape(part)
+    output[...] = output_in[...]
+    hidden_grad[...] = hidden_in[...]
 
 
 def per_device(
@@ -557,29 +827,39 @@
     rank = dt_weight.shape[1]
     state = a_log.shape[1]
     xwidth = x_weight.shape[2]
-    sizes = (half_full, width, slots, padded, half_slots, half_pad, inner_w, rank, state)
-    inner_index = lax.axis_index("inner")
-    inner_count = lax.axis_size("inner")
+    rows_count = lax.axis_size("rows")
+    near = 4 if rows_count % 4 == 0 else 1
+    far = rows_count // near
+    sizes = (
+        half_full, width, slots, padded, half_slots, half_pad, inner_w, rank, state, near, far
+    )
+    wide_tiles = inner_w // 128
+    early_tiles = 2 * (inner_w // BLOCK) * (width // 128)
+    late_rows = width + 2 * xwidth + 2 * rank + 2 * state + BLOCK
+    late_tiles = late_rows // BLOCK * wide_tiles
 
     def shape(*dims, kind=F32):
         return jax.ShapeDtypeStruct(dims, kind)
 
+    vm = pltpu.VMEM
+    sum_outs, sum_scratch = [], []
+    for tiles in (early_tiles, late_tiles):
+        for each, (one, two) in zip(
+            chunk_tiles(tiles, rows_count), ((near, far), (far, near))
+        ):
+            sum_outs.append(shape(one, two, each * BLOCK, 128, kind=BF16))
+            sum_scratch += [
+                vm((one, two, each * BLOCK, 128), BF16),
+                vm((one, two, each * BLOCK, 128), BF16),
+                vm((two, each * BLOCK, 128), BF16),
+                vm((two, each * BLOCK, 128), BF16),
+            ]
     outs = [
         shape(half_slots, width, kind=BF16),
         shape(half_full, width, kind=BF16),
-        shape(1, width),
-        shape(2, width, inner_w),
-        shape(2, 4, inner_w),
-        shape(2, inner_w),
-        shape(2, inner_w, xwidth),
-        shape(2, rank, inner_w),
-        shape(2, inner_w),
-        shape(2, state, inner_w),
-        shape(2, inner_w),
-        shape(inner_w, width),
-        shape(4, inner_w),
+        *sum_outs,
+        shape(8, inner_w),
     ]
-    vm = pltpu.VMEM
     scratch = [
         vm((padded, width), BF16),
         vm((padded, width), BF16),
@@ -593,7 +873,7 @@
         vm((padded, inner_w), F32),
         vm((2, padded, inner_w), F32),
         vm((2, padded, inner_w), BF16),
-        vm((2, inner_w, 128), BF16),
+        vm((2, 128, inner_w), BF16),
         vm((2, 128, inner_w), BF16),
         vm((2, state, inner_w), F32),
         vm((2, state, inner_w), F32),
@@ -639,27 +919,23 @@
         vm((padded, width), BF16),
         vm((padded, width), F32),
         vm((padded, width), BF16),
+        vm((padded, half_full), BF16),
+        vm((padded, 1024), F32),
+        *sum_scratch,
+        vm((8, inner_w), F32),
+        vm((near, 8, inner_w), F32),
+        vm((8, inner_w), F32),
+        vm((far, 8, inner_w), F32),
         pltpu.SemaphoreType.DMA((6,)),
         pltpu.SemaphoreType.DMA((6,)),
+        pltpu.SemaphoreType.DMA((4, 2, near + far - 2)),
+        pltpu.SemaphoreType.DMA((4, 2, near + far - 2)),
+        pltpu.SemaphoreType.DMA((2, near + far - 2)),
     ]
     in_vmem = pl.BlockSpec(memory_space=pltpu.VMEM)
     in_smem = pl.BlockSpec(memory_space=pltpu.SMEM)
     in_specs = [in_vmem, in_vmem, in_smem] + [in_vmem] * 11
-    (
-        output,
-        hidden_grad,
-        gain_whole,
-        in_grad,
-        conv_w_grad,
-        conv_b_grad,
-        xw_grad,
-        dtw_grad,
-        dtb_grad,
-        alog_grad,
-        skip_grad,
-        out_grad,
-        dt_sums,
-    ) = pl.pallas_call(
+    output, hidden_grad, *sums, tiny = pl.pallas_call(
         functools.partial(block_kernel, sizes),
         out_shape=outs,
         in_specs=in_specs,
@@ -672,11 +948,11 @@
         hidden[0],
         kept,
         counts,
-        norm_gain[None],
+        norm_gain,
         in_weight,
         conv_weight,
         conv_bias,
-        x_weight,
+        jnp.swapaxes(x_weight, 1, 2),
         dt_weight,
         dt_bias,
         a_log,
@@ -684,57 +960,34 @@
         out_weight,
         cotangent[0],
     )
-    gain_part = width // inner_count
-    gain_grad = lax.dynamic_slice_in_dim(gain_whole[0], inner_index * gain_part, gain_part, 0)
-    kept_total = jnp.sum(counts).astype(F32)
-    (
-        gain_grad,
-        in_grad,
-        conv_w_grad,
-        conv_b_grad,
-        xw_grad,
-        dtw_grad,
-        dtb_grad,
-        alog_grad,
-        skip_grad,
-        out_grad,
-        dt_sums,
-        kept_total,
-    ) = lax.psum(
-        (
-            gain_grad,
-            in_grad,
-            conv_w_grad,
-            conv_b_grad,
-            xw_grad,
-            dtw_grad,
-            dtb_grad,
-            alog_grad,
-            skip_grad,
-            out_grad,
-            dt_sums,
-            kept_total,
-        ),
-        "rows",
-    )
-    dt_mean = dt_sums[0:2] / kept_total
-    dt_var = dt_sums[2:4] / kept_total - dt_mean * dt_mean
-    return (
-        output[None],
-        hidden_grad[None],
-        gain_grad,
-        in_grad,
-        conv_w_grad,
-        conv_b_grad,
-        xw_grad,
-        dtw_grad,
-        dtb_grad,
-        alog_grad,
-        skip_grad,
-        out_grad,
-        dt_mean,
-        dt_var,
-    )
+    inner_index = lax.axis_index("inner").astype(jnp.int32)[None]
+    outs = [
+        shape(half_slots, width, kind=BF16),
+        shape(half_full, width, kind=BF16),
+        shape(width // lax.axis_size("inner")),
+        shape(2, width, inner_w),
+        shape(2, 4, inner_w),
+        shape(2, inner_w),
+        shape(2, xwidth, inner_w),
+        shape(2, rank, inner_w),
+        shape(2, inner_w),
+        shape(2, state, inner_w),
+        shape(2, inner_w),
+        shape(inner_w, width),
+        shape(2, inner_w),
+        shape(2, inner_w),
+    ]
+    outs = pl.pallas_call(
+        functools.partial(finish_kernel, None),
+        out_shape=outs,
+        in_specs=[in_vmem] * 7 + [in_smem],
+        out_specs=[in_vmem] * len(outs),
+        compiler_params=pltpu.CompilerParams(vmem_limit_bytes=32 * 2**20),
+    )(*sums, tiny, output, hidden_grad, inner_index)
+    outs = list(outs)
+    outs[0], outs[1] = outs[0][None], outs[1][None]
+    outs[6] = jnp.swapaxes(outs[6], 1, 2)
+    return tuple(outs)
 
 
 def solution(mesh):

time: 216 us -> 76.4 us (0.35)
  blocking collectives: 82.3 us -> 0 us
  waiting for transfers between devices: 50.7 us -> 0 us
  between operations: 14.8 us -> 1.32 us
  Pallas kernels: 56.8 us -> 68.2 us
  local copies, waits for them, and re-layouts: 9.53 us -> 6.48 us
    psum x1 -> x0, blocking collectives: 82.3 us -> none  [per_device(): lax.psum((gain_grad, in_grad, conv_w_grad, conv_b_grad, xw_grad, dtw_grad...]
    psum x1 -> x0, waiting for transfers between devices: 50.6 us -> none  [per_device(): lax.psum((gain_grad, in_grad, conv_w_grad, conv_b_grad, xw_grad, dtw_grad...]
    pallas_call x1, Pallas kernels: 56.8 us -> 66.5 us  [per_device(): pl.pallas_call(functools.partial(block_kernel, sizes), out_shape=outs, in...]
    unnamed x31 -> x14, local copies, waits for them, and re-layouts: 8.21 us -> 6.48 us
  transfers between devices with their start and end apart: 1 -> 0, of which waited for: 1 -> 0; matrix products, arithmetic and copies ran while one was open for 1% -> 0% of each run, Pallas kernels for 0% -> 0%
where the time goes in v1:
time: 76.4 us; the launch traced here: 76 us
  Pallas kernels  68.2 us (89%)
  local copies, waits for them, and re-layouts  6.48 us (8%)
  between operations  1.32 us (2%)
    pallas_call x1, Pallas kernels, per_device(): pl.pallas_call(functools.partial(block_kernel, sizes), out_shape=outs, in...  66.5 us
    unnamed x14, local copies, waits for them, and re-layouts  6.48 us
    pallas_call x1, Pallas kernels, per_device(): pl.pallas_call(functools.partial(finish_kernel, None), out_shape=outs, in...  1.62 us

profile of v1, /device:TPU:0, one launch (start us, length us, event | category | flops | bytes accessed | tf_op | source)
XLA Modules:
  0.0 76.0 jit_solution(152860812215702589)
XLA Ops:
  1.3 66.5 %shard_map.245 = (bf16[196,384]{1,0:T(8,128)(2,1)}, bf16[784,384]{1,0:T(8,128)(2,1)}, bf16[4,4,96,128]{3,2,1,0:T(8,128)(2,1)}, bf16[4,4,48,128]{3,2,1,0:T(8,128)...) custom-call(bf16[784,384]{1,0:T(8,128)(2,1)} %bitcast.7, ...), custom_call_target="tpu_custom_call" | custom-call | tf_op jit(solution)/shard_map/pallas_call | solution.py:938
  67.8 0.0 copy-start
  67.9 1.1 %copy-done = bf16[784,384]{1,0:T(8,128)(2,1)S(1)} copy-done((bf16[784,384]{1,0:T(8,128)(2,1)S(1)}, bf16[784,384]{1,0:T(8,128)(2,1)}, u32[]{:S(2)}) %copy-start) | copy-done | bytes 602136
  68.9 0.0 copy-start.1
  68.9 1.0 %copy-done.1 = bf16[4,4,96,128]{3,2,1,0:T(8,128)(2,1)S(1)} copy-done((bf16[4,4,96,128]{3,2,1,0:T(8,128)(2,1)S(1)}, bf16[4,4,96,128]{3,2,1,0:T(8,128)(2,1)}, u32[]{:S(2)}) %copy-start.1) | copy-done | bytes 393240
  69.9 0.0 copy-start.2
  69.9 1.0 %copy-done.2 = bf16[4,4,80,128]{3,2,1,0:T(8,128)(2,1)S(1)} copy-done((bf16[4,4,80,128]{3,2,1,0:T(8,128)(2,1)S(1)}, bf16[4,4,80,128]{3,2,1,0:T(8,128)(2,1)}, u32[]{:S(2)}) %copy-start.2) | copy-done | bytes 327704
  70.9 0.0 copy-start.3
  70.9 0.9 %copy-done.3 = bf16[4,4,48,128]{3,2,1,0:T(8,128)(2,1)S(1)} copy-done((bf16[4,4,48,128]{3,2,1,0:T(8,128)(2,1)S(1)}, bf16[4,4,48,128]{3,2,1,0:T(8,128)(2,1)}, u32[]{:S(2)}) %copy-start.3) | copy-done | bytes 196632
  71.8 0.0 copy-start.4
  71.8 0.9 %copy-done.4 = bf16[196,384]{1,0:T(8,128)(2,1)S(1)} copy-done((bf16[196,384]{1,0:T(8,128)(2,1)S(1)}, bf16[196,384]{1,0:T(8,128)(2,1)}, u32[]{:S(2)}) %copy-start.4) | copy-done | bytes 150552
  72.7 0.0 copy-start.5
  72.7 0.9 %copy-done.5 = bf16[4,4,32,128]{3,2,1,0:T(8,128)(2,1)S(1)} copy-done((bf16[4,4,32,128]{3,2,1,0:T(8,128)(2,1)S(1)}, bf16[4,4,32,128]{3,2,1,0:T(8,128)(2,1)}, u32[]{:S(2)}) %copy-start.5) | copy-done | bytes 131096
  73.6 0.0 copy-start.6
  73.6 0.7 copy-done.6
  74.3 1.6 %shard_map.246 = (bf16[196,384]{1,0:T(8,128)(2,1)}, bf16[784,384]{1,0:T(8,128)(2,1)}, f32[192]{0:T(256)}, f32[2,384,384]{2,1,0:T(8,128)}, f32[2,4,384]{2,1,0:T(4...) custom-call(bf16[4,4,96,128]{3,2,1,0:T(8,128)(2,1)S(1)} %copy-done.1, ...), custom_call_target="tpu_custom_call" | custom-call | tf_op jit(solution)/shard_map/pallas_call | solution.py:980
Async XLA Ops:
  67.8 1.1 %copy-start = (bf16[784,384]{1,0:T(8,128)(2,1)S(1)}, bf16[784,384]{1,0:T(8,128)(2,1)}, u32[]{:S(2)}) copy-start(bf16[784,384]{1,0:T(8,128)(2,1)} %get-tuple-element.41.hidden_in) | copy-start | bytes 1806340
  68.9 1.0 %copy-start.1 = (bf16[4,4,96,128]{3,2,1,0:T(8,128)(2,1)S(1)}, bf16[4,4,96,128]{3,2,1,0:T(8,128)(2,1)}, u32[]{:S(2)}) copy-start(bf16[4,4,96,128]{3,2,1,0:T(8,128)(2,1)} %get-tuple-element.35.early_a) | copy-start | bytes 1179652
  69.9 1.0 %copy-start.2 = (bf16[4,4,80,128]{3,2,1,0:T(8,128)(2,1)S(1)}, bf16[4,4,80,128]{3,2,1,0:T(8,128)(2,1)}, u32[]{:S(2)}) copy-start(bf16[4,4,80,128]{3,2,1,0:T(8,128)(2,1)} %get-tuple-element.37.late_a) | copy-start | bytes 983044
  70.9 0.9 %copy-start.3 = (bf16[4,4,48,128]{3,2,1,0:T(8,128)(2,1)S(1)}, bf16[4,4,48,128]{3,2,1,0:T(8,128)(2,1)}, u32[]{:S(2)}) copy-start(bf16[4,4,48,128]{3,2,1,0:T(8,128)(2,1)} %get-tuple-element.36.early_b) | copy-start | bytes 589828
  71.8 0.9 %copy-start.4 = (bf16[196,384]{1,0:T(8,128)(2,1)S(1)}, bf16[196,384]{1,0:T(8,128)(2,1)}, u32[]{:S(2)}) copy-start(bf16[196,384]{1,0:T(8,128)(2,1)} %get-tuple-element.40.output_in) | copy-start | bytes 451588
  72.7 0.9 %copy-start.5 = (bf16[4,4,32,128]{3,2,1,0:T(8,128)(2,1)S(1)}, bf16[4,4,32,128]{3,2,1,0:T(8,128)(2,1)}, u32[]{:S(2)}) copy-start(bf16[4,4,32,128]{3,2,1,0:T(8,128)(2,1)} %get-tuple-element.38.late_b) | copy-start | bytes 393220
  73.6 0.7 copy-start.6

commit v2 on v1

--- a/solution.py
+++ b/solution.py
@@ -27,6 +27,10 @@
     return lax.dot_general(left, right, (((0,), (0,)), ((), ())), preferred_element_type=F32)
 
 
+def logistic_of(value):
+    return 0.5 * jnp.tanh(0.5 * value) + 0.5
+
+
 def iota(shape, axis):
     return lax.broadcasted_iota(jnp.int32, shape, axis)
 
@@ -36,8 +40,9 @@
 
 
 def chunk_tiles(total, devices):
-    first = -(-2 * total // (3 * devices))
-    return first, max(1, -(-(total - first * devices) // devices))
+    each = -(-total // devices)
+    first = max(1, each * 2 // 3)
+    return first, max(1, each - first)
 
 
 def tile_at(pair, tile):
@@ -150,6 +155,8 @@
     hidden_grad,
     early_a_out,
     early_b_out,
+    mid_a_out,
+    mid_b_out,
     late_a_out,
     late_b_out,
     tiny_out,
@@ -193,8 +200,6 @@
     adj_1,
     car_0,
     car_1,
-    bsum_0,
-    bsum_1,
     csum_0,
     csum_1,
     s1,
@@ -221,6 +226,14 @@
     early_b1,
     early_bm,
     early_b2,
+    mid_a,
+    mid_a1,
+    mid_am,
+    mid_a2,
+    mid_b,
+    mid_b1,
+    mid_bm,
+    mid_b2,
     late_a,
     late_a1,
     late_am,
@@ -236,6 +249,7 @@
     send_sem,
     recv_sem,
     early_sems,
+    mid_sems,
     late_sems,
     tiny_sems,
 ):
@@ -288,6 +302,11 @@
         (early_a, early_a1, early_am, early_a2, early_a_out),
         (early_b, early_b1, early_bm, early_b2, early_b_out),
         early_sems, near, far, my_near, my_far, near_peer, far_peer,
+    )
+    mid = Reducer(
+        (mid_a, mid_a1, mid_am, mid_a2, mid_a_out),
+        (mid_b, mid_b1, mid_bm, mid_b2, mid_b_out),
+        mid_sems, near, far, my_near, my_far, near_peer, far_peer,
     )
     late = Reducer(
         (late_a, late_a1, late_am, late_a2, late_a_out),
@@ -364,7 +383,6 @@
 
     each_block(norm_rows)
     px[8 : 8 + padded, :] = dot(normed[...], in_weight[0])
-    pz[...] = dot(normed[...], in_weight[1])
 
     taps = conv_weight[...].astype(F32)
 
@@ -379,7 +397,7 @@
             for k in range(4):
                 shift = k - 3 if r == 0 else 3 - k
                 total = total + taps[r, k : k + 1, :] * window[8 + shift : 8 + shift + BLOCK, :]
-            logistic = jax.nn.sigmoid(total)
+            logistic = logistic_of(total)
             act[r, rows, :] = (total * logistic * valid).astype(BF16)
             slope[r, rows, :] = logistic * (1.0 + total * (1.0 - logistic)) * valid
 
@@ -388,6 +406,7 @@
     send_part = remote(part, part_in, 2)
     send_part.start()
 
+    pz[...] = dot(normed[...], in_weight[1])
     send_cot.wait()
     gout_f[0:half_pad, :] = cot_pair[0].astype(F32)
     gout_f[half_pad:, :] = jnp.zeros((gout_f.shape[0] - half_pad, width), F32)
@@ -398,7 +417,7 @@
     def gate_rows(block):
         rows = rows_at(block)
         value = pz[rows, :]
-        logistic = jax.nn.sigmoid(value)
+        logistic = logistic_of(value)
         silu = value * logistic
         half_grad = 0.5 * up[rows, :]
         gate[rows, :] = 0.5 * silu
@@ -415,10 +434,16 @@
         rows = rows_at(block)
         low = (part[rows, :] + part_in[rows, :]).astype(BF16)
         projb[rows, :] = low
-        value = low.astype(F32)
-        turned_rows[block] = value.T
 
     each_block(proj_rows)
+    quarter = iota((64, 128), 0) // state
+    start = rank + quarter % 2 * state + quarter // 2 * 64
+    picks = jnp.where(iota((64, 128), 1) == start + iota((64, 128), 0) % state, 1.0, 0.0)
+    picks = picks.astype(BF16)
+
+    turned = dot_nt(picks, projb[...])
+    for block in range(blocks):
+        turned_rows[block] = turned[:, block * BLOCK : block * BLOCK + BLOCK]
     spread_rows[...] = dot(projb[...], sel[...])
 
     def mask_rows(block):
@@ -435,8 +460,7 @@
         for r in range(2):
             pre = sig[r, rows, :] + dt_bias[r : r + 1, :]
             small = jnp.exp(-jnp.abs(pre))
-            inv = 1.0 / (1.0 + small)
-            sig[r, rows, :] = jnp.where(pre >= 0.0, inv, small * inv)
+            sig[r, rows, :] = pre
             soft_plus = jnp.maximum(pre, 0.0) + jnp.log1p(small)
             delta[r, rows, :] = soft_plus
             u[r, rows, :] = soft_plus * act[r, rows, :].astype(F32)
@@ -462,7 +486,7 @@
             held = carry[r]
             block = step if r == 0 else blocks - 1 - step
             base = block * BLOCK
-            b_cols = turned_rows[block, 64 * r + rank : 64 * r + rank + state, :]
+            b_cols = turned_rows[block, 32 * r : 32 * r + state, :]
             for j in range(BLOCK):
                 t = j if r == 0 else BLOCK - 1 - j
                 decay = jnp.exp2(delta[r, pl.ds(base + t, 1), :] * rates2[r])
@@ -485,18 +509,12 @@
         zgrad[rows, :] = (summed * zslope[rows, :]).astype(BF16)
 
     each_block(mix_rows)
-    terms[0:padded, :] = dot(gated[...], out_weight[...])
-    terms_pair[0] = terms[0:half_pad, :]
-    terms_pair[1] = terms[half_slots : half_slots + half_pad, :]
-    send_terms = remote(terms_pair.at[peer], terms_in, 3)
-    send_terms.start()
     early.put(0, dot_tn(gated[...], gout[...]))
     early.put(inner_w // BLOCK * (width // 128), dot_tn(normed[...], zgrad[...]))
     early.first()
-    npart[...] = dot_nt(zgrad[...], in_weight[1])
 
     adj_refs, car_refs = (adj_0, adj_1), (car_0, car_1)
-    bsum_refs, csum_refs = (bsum_0, bsum_1), (csum_0, csum_1)
+    csum_refs = (csum_0, csum_1)
     block_mask = diagonal[:, 0:256]
     ones_block = block_mask.astype(BF16)
     ones_rows = jnp.ones((BLOCK, 128), BF16)
@@ -513,7 +531,7 @@
             rows = rows_at(block)
             s1[r, rows, :] = dot(blkm[rows, 512 * r : 512 * r + 256], adj_refs[r][...])
             cas[r, rows, :] = dot(ones_block, car_refs[r][...])
-            b_sums = dot_nt(ones_rows, bsum_refs[r][...])
+            b_sums = dot_nt(u[r, rows, :].astype(BF16), adj_refs[r][...])
             c_sums = dot_nt(ones_rows, csum_refs[r][...])
             pgm[rows, 512 * r : 512 * r + 256] = (b_sums * block_mask).astype(BF16)
             pgm[rows, 512 * r + 256 : 512 * r + 512] = (c_sums * block_mask).astype(BF16)
@@ -525,7 +543,7 @@
             passed, rate_sum, after = carry[r]
             block = blocks - 1 - step if r == 0 else step
             base = block * BLOCK
-            c_cols = turned_rows[block, 64 * r + rank + state : 64 * r + rank + 2 * state, :]
+            c_cols = turned_rows[block, 32 * r + state : 32 * r + 2 * state, :]
             for j in range(BLOCK):
                 t = BLOCK - 1 - j if r == 0 else j
                 own = slice(t * 16, t * 16 + 16)
@@ -540,7 +558,6 @@
                 carried = passed * before
                 car_refs[r][own, :] = (carried * rates[r]).astype(BF16)
                 rate_sum = rate_sum + carried * step_size
-                bsum_refs[r][own, :] = fold_lanes(adjoint * u[r, pl.ds(base + t, 1), :])
                 csum_refs[r][own, :] = fold_lanes(after * upstream)
                 after = before
             out.append((passed, rate_sum, after))
@@ -548,7 +565,7 @@
 
     last = states[0, padded * 16 : padded * 16 + 16, :].astype(F32)
     top = states[1, 0:16, :].astype(F32)
-    cuts = [0, blocks * 2 // 5, blocks * 7 // 10, blocks]
+    cuts = [0, blocks * 12 // 25, blocks * 21 // 25, blocks]
     final = ((zero_state, zero_state, last), (zero_state, zero_state, top))
     final = lax.fori_loop(cuts[0], cuts[1], backward_step, final)
     early.second()
@@ -556,13 +573,10 @@
     early.third()
     final = lax.fori_loop(cuts[2], cuts[3], backward_step, final)
     emit_back(blocks - 1)
-    early.fourth()
     wide_tiles = inner_w // 128
-    at_xw = width // BLOCK * wide_tiles
-    at_dtw = at_xw + 2 * (rank + 2 * state) // BLOCK * wide_tiles
+    at_dtw = 2 * (rank + 2 * state) // BLOCK * wide_tiles
     at_alog = at_dtw + 2 * rank // BLOCK * wide_tiles
     at_small = at_alog + 2 * state // BLOCK * wide_tiles
-    late.put(at_alog, jnp.concatenate([final[r][1] * rates[r] for r in range(2)], 0))
 
     def soft_rows(block, carry):
         rows = rows_at(block)
@@ -575,7 +589,7 @@
             active = act[r, rows, :].astype(F32)
             step_size = delta[r, rows, :]
             first_sum = s1[r, rows, :]
-            pre_grad = (active * first_sum + cas[r, rows, :]) * sig[r, rows, :]
+            pre_grad = (active * first_sum + cas[r, rows, :]) * jnp.exp(sig[r, rows, :] - step_size)
             soft[r, rows, :] = pre_grad.astype(BF16)
             actg[r, rows, :] = first_sum * step_size + skip_gain[r : r + 1, :] * upstream
             kept_step = jnp.where(valid, step_size, 0.0)
@@ -590,36 +604,15 @@
         return tuple(out)
 
     wide = jnp.zeros((BLOCK, inner_w), F32)
-    sums = lax.fori_loop(0, blocks, soft_rows, ((wide,) * 4,) * 2)
+    sums = lax.fori_loop(0, blocks, soft_rows, ((wide,) * 4,) * 2, unroll=5)
     pgrad[...] = (
         dot_nt(pgm[...], sel[...]) + dot_nt(soft[0], dtw_pad[0]) + dot_nt(soft[1], dtw_pad[1])
     )
     send_pgrad = remote(pgrad, pgrad_in, 4)
     send_pgrad.start()
-    def total(value):
-        return jnp.sum(value, axis=0, keepdims=True)
-
-    low_grads = [
-        dot_tn(projb[...], soft[r])[64 * r : 64 * r + rank, :] for r in range(2)
-    ]
-    late.put(at_dtw, jnp.concatenate(low_grads, 0))
-    for r in range(2):
-        tiny[r : r + 1, :] = total(sums[r][2])
-        tiny[2 + r : 3 + r, :] = total(sums[r][3])
-    tiny[5:8, :] = jnp.full((3, inner_w), count.astype(F32))
-
-    send_terms.wait()
-    gathered_half = jnp.where(
-        inner == 0, gathered[0:half_slots, :], gathered[half_slots : 2 * half_slots, :]
-    )
-    mixer = terms_pair[inner][0:half_slots, :] + terms_in[0:half_slots, :]
-    output[...] = jnp.where(cot_rows < count, gathered_half + mixer, 0.0).astype(BF16)
-
+    early.fourth()
     send_pgrad.wait()
     pgb[...] = (pgrad[...] + pgrad_in[...]).astype(BF16)
-    xwidth = rank + 2 * state
-    xw_grads = [dot_tn(pgb[...], act[r])[64 * r : 64 * r + xwidth, :] for r in range(2)]
-    late.put(at_xw, jnp.concatenate(xw_grads, 0))
     for r in range(2):
         actg[r] = actg[r] + dot(pgb[...], xw_cat[r])
 
@@ -631,33 +624,64 @@
 
     each_block(back_rows)
 
-    def conv_back_rows(block, carry):
+    def conv_back_rows(block):
         base = pl.multiple_of(block * BLOCK, BLOCK)
-        window = px[pl.ds(base, BLOCK + 16), :]
         total = jnp.zeros((BLOCK, inner_w), F32)
-        out = []
         for r in range(2):
             grads = cgrad[r, pl.ds(base, BLOCK + 16), :]
-            here = grads[8 : 8 + BLOCK, :]
             for k in range(4):
                 shift = k - 3 if r == 0 else 3 - k
                 total = total + taps[r, k : k + 1, :] * grads[8 - shift : 8 - shift + BLOCK, :]
+        xgrad[rows_at(block), :] = total.astype(BF16)
+
+    each_block(conv_back_rows)
+    late.put(0, dot_tn(normed[...], xgrad[...]))
+    late.first()
+    npart[...] = dot_nt(xgrad[...], in_weight[0]) + dot_nt(zgrad[...], in_weight[1])
+    send_npart = remote(npart, npart_in, 5)
+    send_npart.start()
+    terms[0:padded, :] = dot(gated[...], out_weight[...])
+    terms_pair[0] = terms[0:half_pad, :]
+    terms_pair[1] = terms[half_slots : half_slots + half_pad, :]
+    send_terms = remote(terms_pair.at[peer], terms_in, 3)
+    send_terms.start()
+
+    def conv_sum_rows(block, carry):
+        base = pl.multiple_of(block * BLOCK, BLOCK)
+        window = px[pl.ds(base, BLOCK + 16), :]
+        out = []
+        for r in range(2):
+            here = cgrad[r, pl.ds(base + 8, BLOCK), :]
+            for k in range(4):
+                shift = k - 3 if r == 0 else 3 - k
                 out.append(carry[5 * r + k] + here * window[8 + shift : 8 + shift + BLOCK, :])
             out.append(carry[5 * r + 4] + here)
-        xgrad[rows_at(block), :] = total.astype(BF16)
         return tuple(out)
 
-    conv_sums = lax.fori_loop(0, blocks, conv_back_rows, (wide,) * 10)
-    late.put(0, dot_tn(normed[...], xgrad[...]))
+    conv_sums = lax.fori_loop(0, blocks, conv_sum_rows, (wide,) * 10)
+
+    def total(value):
+        return jnp.sum(value, axis=0, keepdims=True)
+
+    low_grads = [
+        dot_tn(projb[...], soft[r])[64 * r : 64 * r + rank, :] for r in range(2)
+    ]
+    mid.put(at_dtw, jnp.concatenate(low_grads, 0))
+    for r in range(2):
+        tiny[r : r + 1, :] = total(sums[r][2])
+        tiny[2 + r : 3 + r, :] = total(sums[r][3])
+    tiny[5:8, :] = jnp.full((3, inner_w), count.astype(F32))
     small = [total(conv_sums[5 * r + k]) for r in range(2) for k in range(4)]
     small += [total(conv_sums[5 * r + 4]) for r in range(2)]
     small += [total(sums[r][i]) for i in range(2) for r in range(2)]
     small += [jnp.zeros((BLOCK - len(small), inner_w), F32)]
-    late.put(at_small, jnp.concatenate(small, 0))
-    late.first()
-    npart[...] = npart[...] + dot_nt(xgrad[...], in_weight[0])
-    send_npart = remote(npart, npart_in, 5)
-    send_npart.start()
+    mid.put(at_small, jnp.concatenate(small, 0))
+    xwidth = rank + 2 * state
+    xw_grads = [dot_tn(pgb[...], act[r])[64 * r : 64 * r + xwidth, :] for r in range(2)]
+    mid.put(0, jnp.concatenate(xw_grads, 0))
+
+    mid.put(at_alog, jnp.concatenate([final[r][1] * rates[r] for r in range(2)], 0))
+    mid.first()
 
     send_npart.wait()
 
@@ -696,6 +720,15 @@
 
     copies = tiny_sends(tiny, tiny_low, near_peer, my_near, near, 0)
     late.second()
+    mid.second()
+
+    send_terms.wait()
+    gathered_half = jnp.where(
+        inner == 0, gathered[0:half_slots, :], gathered[half_slots : 2 * half_slots, :]
+    )
+    mixer = terms_pair[inner][0:half_slots, :] + terms_in[0:half_slots, :]
+    output[...] = jnp.where(cot_rows < count, gathered_half + mixer, 0.0).astype(BF16)
+
 
     slot_lane = iota((1, slots), 1)
     places = jnp.where(slot_lane < count, kept_row - first, -1.0)
@@ -717,6 +750,7 @@
     tiny_mid[...] = held
     copies = tiny_sends(tiny_mid, tiny_high, far_peer, my_far, far, near - 1)
     late.third()
+    mid.third()
     for copy in copies:
         copy.wait()
     held = tiny_mid[...]
@@ -724,7 +758,9 @@
         held = held + tiny_high[lax.rem(my_far + offset, far)]
     tiny_out[...] = held
     late.fourth()
+    mid.fourth()
     early.finish()
+    mid.finish()
     late.finish()
 
 
@@ -732,6 +768,8 @@
     tiles,
     early_a,
     early_b,
+    mid_a,
+    mid_b,
     late_a,
     late_b,
     tiny,
@@ -768,24 +806,23 @@
             parts.append(jnp.concatenate(line, 1))
         return jnp.concatenate(parts, 0).astype(F32)
 
-    early, late = (early_a, early_b), (late_a, late_b)
+    early, mid, late = (early_a, early_b), (mid_a, mid_b), (late_a, late_b)
     out_grad[...] = take(early, 0, inner_w, width)
     in_grad[1] = take(early, inner_w // BLOCK * (width // 128), width, inner_w)
     in_grad[0] = take(late, 0, width, inner_w)
-    at = width // BLOCK * wide_tiles
-    both = take(late, at, 2 * xwidth, inner_w)
+    both = take(mid, 0, 2 * xwidth, inner_w)
     for r in range(2):
         xw_grad[r] = both[r * xwidth : (r + 1) * xwidth, :]
-    at += 2 * xwidth // BLOCK * wide_tiles
-    both = take(late, at, 2 * rank, inner_w)
+    at = 2 * xwidth // BLOCK * wide_tiles
+    both = take(mid, at, 2 * rank, inner_w)
     for r in range(2):
         dtw_grad[r] = both[r * rank : (r + 1) * rank, :]
     at += 2 * rank // BLOCK * wide_tiles
-    both = take(late, at, 2 * state, inner_w)
+    both = take(mid, at, 2 * state, inner_w)
     for r in range(2):
         alog_grad[r] = both[r * state : (r + 1) * state, :]
     at += 2 * state // BLOCK * wide_tiles
-    small = take(late, at, BLOCK, inner_w)
+    small = take(mid, at, BLOCK, inner_w)
     for r in range(2):
         conv_w_grad[r] = small[4 * r : 4 * r + 4, :]
     conv_b_grad[...] = small[8:10, :]
@@ -835,15 +872,15 @@
     )
     wide_tiles = inner_w // 128
     early_tiles = 2 * (inner_w // BLOCK) * (width // 128)
-    late_rows = width + 2 * xwidth + 2 * rank + 2 * state + BLOCK
-    late_tiles = late_rows // BLOCK * wide_tiles
+    mid_tiles = (2 * xwidth + 2 * rank + 2 * state + BLOCK) // BLOCK * wide_tiles
+    late_tiles = width // BLOCK * wide_tiles
 
     def shape(*dims, kind=F32):
         return jax.ShapeDtypeStruct(dims, kind)
 
     vm = pltpu.VMEM
     sum_outs, sum_scratch = [], []
-    for tiles in (early_tiles, late_tiles):
+    for tiles in (early_tiles, mid_tiles, late_tiles):
         for each, (one, two) in zip(
             chunk_tiles(tiles, rows_count), ((near, far), (far, near))
         ):
@@ -893,7 +930,7 @@
         vm((2, half_pad, width), F32),
         vm((half_pad, width), F32),
         vm((padded, 1024), BF16),
-        vm((padded // BLOCK, 128, BLOCK), F32),
+        vm((padded // BLOCK, 64, BLOCK), F32),
         vm((128, 1024), BF16),
         vm((2, padded * 16 + 16, inner_w), BF16),
         vm((2, padded, inner_w), F32),
@@ -901,8 +938,6 @@
         vm((256, inner_w), BF16),
         vm((256, inner_w), BF16),
         vm((256, inner_w), BF16),
-        vm((256, 128), BF16),
-        vm((256, 128), BF16),
         vm((256, 128), BF16),
         vm((256, 128), BF16),
         vm((2, padded, inner_w), F32),
@@ -928,6 +963,7 @@
         vm((far, 8, inner_w), F32),
         pltpu.SemaphoreType.DMA((6,)),
         pltpu.SemaphoreType.DMA((6,)),
+        pltpu.SemaphoreType.DMA((4, 2, near + far - 2)),
         pltpu.SemaphoreType.DMA((4, 2, near + far - 2)),
         pltpu.SemaphoreType.DMA((4, 2, near + far - 2)),
         pltpu.SemaphoreType.DMA((2, near + far - 2)),
@@ -980,9 +1016,9 @@
     outs = pl.pallas_call(
         functools.partial(finish_kernel, None),
         out_shape=outs,
-        in_specs=[in_vmem] * 7 + [in_smem],
+        in_specs=[in_vmem] * 9 + [in_smem],
         out_specs=[in_vmem] * len(outs),
-        compiler_params=pltpu.CompilerParams(vmem_limit_bytes=32 * 2**20),
+        compiler_params=pltpu.CompilerParams(vmem_limit_bytes=63 * 2**20),
     )(*sums, tiny, output, hidden_grad, inner_index)
     outs = list(outs)
     outs[0], outs[1] = outs[0][None], outs[1][None]

time: 76.4 us -> 66.3 us (0.87)
  local copies, waits for them, and re-layouts: 6.48 us -> 0 us
  Pallas kernels: 68.2 us -> 64.8 us
    unnamed x14 -> x0, local copies, waits for them, and re-layouts: 6.48 us -> none
    pallas_call x1, Pallas kernels: 66.5 us -> 61.6 us  [per_device(): pl.pallas_call(functools.partial(block_kernel, sizes), out_shape=outs, in...]
    pallas_call x1, Pallas kernels: 1.62 us -> 3.18 us  [per_device(): pl.pallas_call(functools.partial(finish_kernel, None), out_shape=outs, in...]
where the time goes in v2:
time: 66.3 us; the launch traced here: 66.1 us
  Pallas kernels  64.8 us (98%)
  between operations  1.31 us (2%)
    pallas_call x1, Pallas kernels, per_device(): pl.pallas_call(functools.partial(block_kernel, sizes), out_shape=outs, in...  61.6 us
    pallas_call x1, Pallas kernels, per_device(): pl.pallas_call(functools.partial(finish_kernel, None), out_shape=outs, in...  3.18 us

profile of v2, /device:TPU:0, one launch (start us, length us, event | category | flops | bytes accessed | tf_op | source)
XLA Modules:
  0.0 66.1 jit_solution(12015472398649533755)
XLA Ops:
  1.3 61.6 %shard_map.245 = (bf16[196,384]{1,0:T(8,128)(2,1)}, bf16[784,384]{1,0:T(8,128)(2,1)}, bf16[4,4,96,128]{3,2,1,0:T(8,128)(2,1)}, bf16[4,4,48,128]{3,2,1,0:T(8,128)...) custom-call(bf16[784,384]{1,0:T(8,128)(2,1)} %bitcast.7, ...), custom_call_target="tpu_custom_call" | custom-call | tf_op jit(solution)/shard_map/pallas_call | solution.py:974
  62.9 3.2 %shard_map.246 = (bf16[196,384]{1,0:T(8,128)(2,1)}, bf16[784,384]{1,0:T(8,128)(2,1)}, f32[192]{0:T(256)}, f32[2,384,384]{2,1,0:T(8,128)}, f32[2,4,384]{2,1,0:T(4...) custom-call(bf16[4,4,96,128]{3,2,1,0:T(8,128)(2,1)} %get-tuple-eleme, ...), custom_call_target="tpu_custom_call" | custom-call | tf_op jit(solution)/shard_map/pallas_call | solution.py:1016

commit v3 on v2

--- a/solution.py
+++ b/solution.py
@@ -56,6 +56,34 @@
     return ref, (outer, middle, slice(place * BLOCK, place * BLOCK + BLOCK), slice(None))
 
 
+def put_tiles(place, value):
+    columns = value.shape[1] // 128
+    for tile in range(value.shape[0] // BLOCK):
+        for lane in range(columns):
+            ref, at = place(tile * columns + lane)
+            part = value[tile * BLOCK : tile * BLOCK + BLOCK, lane * 128 : lane * 128 + 128]
+            ref[at] = part.astype(BF16)
+
+
+def small_place(late, mid, counts, first):
+    whole, spare, _ = counts
+
+    def place(tile):
+        tile += first
+        if tile < spare:
+            return tile_at(late, whole + tile)
+        return tile_at(mid, tile - spare)
+
+    return place
+
+
+def small_tiles(width, wide_tiles, rank, state):
+    late = width // BLOCK * wide_tiles
+    small = (2 * state + 2 * rank + 2 * (rank + 2 * state) + BLOCK) // BLOCK * wide_tiles
+    spare = min(8, small)
+    return late, spare, small - spare
+
+
 class Reducer:
     def __init__(self, a, b, sems, near, far, my_near, my_far, near_peer, far_peer):
         self.ways = [
@@ -63,76 +91,98 @@
             (b, (far, my_far, far_peer), (near, my_near, near_peer)),
         ]
         self.sems = sems
-        self.copies = []
+        self.copies = [[], []]
+
+    def sources(self):
+        return (self.ways[0][0][0], self.ways[1][0][0])
 
     def put(self, first, value):
-        columns = value.shape[1] // 128
-        pair = (self.ways[0][0][0], self.ways[1][0][0])
-        for tile in range(value.shape[0] // BLOCK):
-            for lane in range(columns):
-                ref, at = tile_at(pair, first + tile * columns + lane)
-                part = value[tile * BLOCK : tile * BLOCK + BLOCK, lane * 128 : lane * 128 + 128]
-                ref[at] = part.astype(BF16)
-
-    def send(self, phase, make):
-        self.copies = []
-        place = 0
-        for refs, one, two in self.ways:
-            number, mine, peer_of = one if phase in (0, 3) else two
-            for offset in range(1, number):
-                source, target = make(refs, one, two, lax.rem(mine + offset, number))
-                copy = pltpu.make_async_remote_copy(
+        put_tiles(lambda tile: tile_at(self.sources(), first + tile), value)
+
+    def send(self, way, phase, make):
+        refs, one, two = self.ways[way]
+        number, mine, peer_of = one if phase in (0, 3) else two
+        copies = []
+        for offset in range(1, number):
+            source, target = make(lax.rem(mine + offset, number))
+            copies.append(
+                pltpu.make_async_remote_copy(
                     src_ref=source,
                     dst_ref=target,
-                    send_sem=self.sems.at[phase, 0, place],
-                    recv_sem=self.sems.at[phase, 1, place],
+                    send_sem=self.sems.at[phase, 0, way, offset - 1],
+                    recv_sem=self.sems.at[phase, 1, way, offset - 1],
                     device_id={"rows": peer_of(offset)},
                     device_id_type=MESH,
                 )
-                copy.start()
-                self.copies.append(copy)
-                place += 1
-
-    def wait(self):
-        for copy in self.copies:
+            )
+            copies[-1].start()
+        self.copies[way] = copies
+
+    def wait(self, way):
+        for copy in self.copies[way]:
             copy.wait()
 
     def first(self):
-        self.send(0, lambda refs, one, two, other: (refs[0].at[other], refs[1].at[one[1]]))
+        for way, (refs, one, two) in enumerate(self.ways):
+            self.send(way, 0, lambda other: (refs[0].at[other], refs[1].at[one[1]]))
 
     def second(self):
-        self.wait()
-        for refs, one, two in self.ways:
+        for way, (refs, one, two) in enumerate(self.ways):
+            self.wait(way)
             number, mine, _ = one
             for part in range(two[0]):
                 held = refs[0][mine, part].astype(F32)
                 for offset in range(1, number):
                     held = held + refs[1][lax.rem(mine + offset, number), part].astype(F32)
                 refs[2][part] = held.astype(BF16)
-        self.send(1, lambda refs, one, two, other: (refs[2].at[other], refs[3].at[two[1]]))
+            self.send(way, 1, lambda other: (refs[2].at[other], refs[3].at[two[1]]))
 
     def third(self):
-        self.wait()
-        for refs, one, two in self.ways:
+        for way, (refs, one, two) in enumerate(self.ways):
+            self.wait(way)
             number, mine, _ = two
             held = refs[2][mine].astype(F32)
             for offset in range(1, number):
                 held = held + refs[3][lax.rem(mine + offset, number)].astype(F32)
             refs[4][one[1], mine] = held.astype(BF16)
-        self.send(
-            2,
-            lambda refs, one, two, other: (
-                refs[4].at[one[1], two[1]],
-                refs[4].at[one[1], two[1]],
-            ),
-        )
+            whole = refs[4].at[one[1], mine]
+            self.send(way, 2, lambda other: (whole, whole))
 
     def fourth(self):
-        self.wait()
-        self.send(3, lambda refs, one, two, other: (refs[4].at[one[1]], refs[4].at[one[1]]))
+        for way in (1, 0):
+            refs, one, two = self.ways[way]
+            self.wait(way)
+            whole = refs[4].at[one[1]]
+            self.send(way, 3, lambda other: (whole, whole))
 
     def finish(self):
-        self.wait()
+        self.wait(0)
+        self.wait(1)
+
+
+class ShortReducer(Reducer):
+    def second(self):
+        for way, (refs, one, two) in enumerate(self.ways):
+            self.wait(way)
+            number, mine, _ = one
+            for part in range(two[0]):
+                held = refs[0][mine, part].astype(F32)
+                for offset in range(1, number):
+                    held = held + refs[1][lax.rem(mine + offset, number), part].astype(F32)
+                refs[2][part] = held.astype(BF16)
+            self.send(way, 1, lambda other: (refs[2], refs[3].at[two[1]]))
+            refs[3][pl.ds(two[1], 1)] = refs[2][...][None]
+
+    def third(self):
+        for way, (refs, one, two) in enumerate(self.ways):
+            self.wait(way)
+            for part in range(two[0]):
+                held = refs[3][0, part].astype(F32)
+                for other in range(1, two[0]):
+                    held = held + refs[3][other, part].astype(F32)
+                refs[4][one[1], part] = held.astype(BF16)
+            whole = refs[4].at[one[1]]
+            self.send(way, 3, lambda other: (whole, whole))
 
 
 def block_kernel(
@@ -195,6 +245,7 @@
     turned_rows,
     sel,
     states,
+    recent,
     ys,
     adj_0,
     adj_1,
@@ -303,7 +354,7 @@
         (early_b, early_b1, early_bm, early_b2, early_b_out),
         early_sems, near, far, my_near, my_far, near_peer, far_peer,
     )
-    mid = Reducer(
+    mid = ShortReducer(
         (mid_a, mid_a1, mid_am, mid_a2, mid_a_out),
         (mid_b, mid_b1, mid_bm, mid_b2, mid_b_out),
         mid_sems, near, far, my_near, my_far, near_peer, far_peer,
@@ -333,13 +384,12 @@
         column = iota((BLOCK, half_full), 1).astype(F32)
         chosen[rows_at(block), :] = jnp.where(place == column, 1.0, 0.0).astype(BF16)
 
-    each_block(pick_rows)
+    each_block(pick_rows, 25)
     picked[...] = dot(chosen[...], hidden[...]).astype(BF16)
     pl.semaphore_wait(barrier, near + far - 1)
     send_pick = remote(picked, picked_in, 0)
     send_pick.start()
     send_cot = remote(cot_pair.at[inner], cot_pair.at[inner], 1)
-    send_cot.start()
 
     def at_rows(value, r):
         parts = [value, jnp.zeros((128 - 64 * r - value.shape[0], inner_w), F32)]
@@ -371,6 +421,7 @@
     states[1, padded * 16 : padded * 16 + 16, :] = jnp.zeros((16, inner_w), BF16)
 
     send_pick.wait()
+    send_cot.start()
     gain = norm_gain[...].reshape(1, width)
 
     def norm_rows(block):
@@ -386,22 +437,24 @@
 
     taps = conv_weight[...].astype(F32)
 
-    def conv_rows(block):
-        base = pl.multiple_of(block * BLOCK, BLOCK)
-        rows = rows_at(block)
-        slot = iota((BLOCK, 1), 0) + block * BLOCK
-        valid = jnp.where(slot < count, 1.0, 0.0)
-        window = px[pl.ds(base, BLOCK + 16), :]
+    span = 80
+
+    def conv_rows(step, carry):
+        base = pl.multiple_of(step * span, BLOCK)
+        rows = pl.ds(base, span)
+        valid = jnp.where(iota((span, 1), 0) + step * span < count, 1.0, 0.0)
+        window = px[pl.ds(base, span + 16), :]
         for r in range(2):
             total = conv_bias[r : r + 1, :]
             for k in range(4):
                 shift = k - 3 if r == 0 else 3 - k
-                total = total + taps[r, k : k + 1, :] * window[8 + shift : 8 + shift + BLOCK, :]
+                total = total + taps[r, k : k + 1, :] * window[8 + shift : 8 + shift + span, :]
             logistic = logistic_of(total)
             act[r, rows, :] = (total * logistic * valid).astype(BF16)
             slope[r, rows, :] = logistic * (1.0 + total * (1.0 - logistic)) * valid
-
-    each_block(conv_rows)
+        return carry
+
+    lax.fori_loop(0, padded // span, conv_rows, 0)
     part[...] = dot_nt(act[0], xw_cat[0]) + dot_nt(act[1], xw_cat[1])
     send_part = remote(part, part_in, 2)
     send_part.start()
@@ -473,8 +526,7 @@
     def emit_y(step):
         for r in range(2):
             block = step if r == 0 else blocks - 1 - step
-            first_row = block * 256 + (16 if r == 0 else 0)
-            held = states[r, pl.ds(pl.multiple_of(first_row, 16), 256), :]
+            held = recent[r]
             ys[r, rows_at(block), :] = dot(
                 blkm[rows_at(block), 512 * r + 256 : 512 * r + 512], held
             )
@@ -492,7 +544,9 @@
                 decay = jnp.exp2(delta[r, pl.ds(base + t, 1), :] * rates2[r])
                 b_wide = jnp.broadcast_to(b_cols[:, t : t + 1], (state, inner_w))
                 held = decay * held + u[r, pl.ds(base + t, 1), :] * b_wide
-                states[r, state_rows(base + t + (1 if r == 0 else 0)), :] = held.astype(BF16)
+                low = held.astype(BF16)
+                states[r, state_rows(base + t + (1 if r == 0 else 0)), :] = low
+                recent[r, t * 16 : t * 16 + 16, :] = low
             out.append(held)
         return tuple(out)
 
@@ -574,9 +628,13 @@
     final = lax.fori_loop(cuts[2], cuts[3], backward_step, final)
     emit_back(blocks - 1)
     wide_tiles = inner_w // 128
-    at_dtw = 2 * (rank + 2 * state) // BLOCK * wide_tiles
-    at_alog = at_dtw + 2 * rank // BLOCK * wide_tiles
-    at_small = at_alog + 2 * state // BLOCK * wide_tiles
+    at_dtw = 2 * state // BLOCK * wide_tiles
+    at_xw = at_dtw + 2 * rank // BLOCK * wide_tiles
+    at_small = at_xw + 2 * (rank + 2 * state) // BLOCK * wide_tiles
+    tile_counts = small_tiles(width, wide_tiles, rank, state)
+
+    def put_small(first, value):
+        put_tiles(small_place(late.sources(), mid.sources(), tile_counts, first), value)
 
     def soft_rows(block, carry):
         rows = rows_at(block)
@@ -611,18 +669,16 @@
     send_pgrad = remote(pgrad, pgrad_in, 4)
     send_pgrad.start()
     early.fourth()
+    low_grads = [
+        dot_tn(projb[...], soft[r])[64 * r : 64 * r + rank, :] for r in range(2)
+    ]
+    put_small(at_dtw, jnp.concatenate(low_grads, 0))
+    put_small(0, jnp.concatenate([final[r][1] * rates[r] for r in range(2)], 0))
     send_pgrad.wait()
     pgb[...] = (pgrad[...] + pgrad_in[...]).astype(BF16)
     for r in range(2):
-        actg[r] = actg[r] + dot(pgb[...], xw_cat[r])
-
-    def back_rows(block):
-        rows = rows_at(block)
-        inside = pl.ds(pl.multiple_of(block * BLOCK, BLOCK) + 8, BLOCK)
-        for r in range(2):
-            cgrad[r, inside, :] = actg[r, rows, :] * slope[r, rows, :]
-
-    each_block(back_rows)
+        inside = slice(8, 8 + padded)
+        cgrad[r, inside, :] = (actg[r] + dot(pgb[...], xw_cat[r])) * slope[r]
 
     def conv_back_rows(block):
         base = pl.multiple_of(block * BLOCK, BLOCK)
@@ -658,15 +714,11 @@
             out.append(carry[5 * r + 4] + here)
         return tuple(out)
 
-    conv_sums = lax.fori_loop(0, blocks, conv_sum_rows, (wide,) * 10)
+    conv_sums = lax.fori_loop(0, blocks, conv_sum_rows, (wide,) * 10, unroll=5)
 
     def total(value):
         return jnp.sum(value, axis=0, keepdims=True)
 
-    low_grads = [
-        dot_tn(projb[...], soft[r])[64 * r : 64 * r + rank, :] for r in range(2)
-    ]
-    mid.put(at_dtw, jnp.concatenate(low_grads, 0))
     for r in range(2):
         tiny[r : r + 1, :] = total(sums[r][2])
         tiny[2 + r : 3 + r, :] = total(sums[r][3])
@@ -675,12 +727,11 @@
     small += [total(conv_sums[5 * r + 4]) for r in range(2)]
     small += [total(sums[r][i]) for i in range(2) for r in range(2)]
     small += [jnp.zeros((BLOCK - len(small), inner_w), F32)]
-    mid.put(at_small, jnp.concatenate(small, 0))
+    put_small(at_small, jnp.concatenate(small, 0))
     xwidth = rank + 2 * state
     xw_grads = [dot_tn(pgb[...], act[r])[64 * r : 64 * r + xwidth, :] for r in range(2)]
-    mid.put(0, jnp.concatenate(xw_grads, 0))
-
-    mid.put(at_alog, jnp.concatenate([final[r][1] * rates[r] for r in range(2)], 0))
+    put_small(at_xw, jnp.concatenate(xw_grads, 0))
+
     mid.first()
 
     send_npart.wait()
@@ -758,7 +809,6 @@
         held = held + tiny_high[lax.rem(my_far + offset, far)]
     tiny_out[...] = held
     late.fourth()
-    mid.fourth()
     early.finish()
     mid.finish()
     late.finish()
@@ -797,11 +847,14 @@
     wide_tiles = inner_w // 128
 
     def take(pair, first, rows, columns):
+        return take_tiles(lambda tile: tile_at(pair, first + tile), rows, columns)
+
+    def take_tiles(place, rows, columns):
         parts = []
         for tile in range(rows // BLOCK):
             line = []
             for lane in range(columns // 128):
-                ref, at = tile_at(pair, first + tile * (columns // 128) + lane)
+                ref, at = place(tile * (columns // 128) + lane)
                 line.append(ref[at])
             parts.append(jnp.concatenate(line, 1))
         return jnp.concatenate(parts, 0).astype(F32)
@@ -810,19 +863,21 @@
     out_grad[...] = take(early, 0, inner_w, width)
     in_grad[1] = take(early, inner_w // BLOCK * (width // 128), width, inner_w)
     in_grad[0] = take(late, 0, width, inner_w)
-    both = take(mid, 0, 2 * xwidth, inner_w)
-    for r in range(2):
-        xw_grad[r] = both[r * xwidth : (r + 1) * xwidth, :]
-    at = 2 * xwidth // BLOCK * wide_tiles
-    both = take(mid, at, 2 * rank, inner_w)
-    for r in range(2):
-        dtw_grad[r] = both[r * rank : (r + 1) * rank, :]
-    at += 2 * rank // BLOCK * wide_tiles
-    both = take(mid, at, 2 * state, inner_w)
-    for r in range(2):
-        alog_grad[r] = both[r * state : (r + 1) * state, :]
-    at += 2 * state // BLOCK * wide_tiles
-    small = take(mid, at, BLOCK, inner_w)
+    tile_counts = small_tiles(width, wide_tiles, rank, state)
+    at = 0
+
+    def take_small(rows):
+        nonlocal at
+        value = take_tiles(small_place(late, mid, tile_counts, at), rows, inner_w)
+        at += rows // BLOCK * wide_tiles
+        return value
+
+    for ref in (alog_grad, dtw_grad, xw_grad):
+        each = ref.shape[1]
+        both = take_small(2 * each)
+        for r in range(2):
+            ref[r] = both[r * each : (r + 1) * each, :]
+    small = take_small(BLOCK)
     for r in range(2):
         conv_w_grad[r] = small[4 * r : 4 * r + 4, :]
     conv_b_grad[...] = small[8:10, :]
@@ -872,15 +927,15 @@
     )
     wide_tiles = inner_w // 128
     early_tiles = 2 * (inner_w // BLOCK) * (width // 128)
-    mid_tiles = (2 * xwidth + 2 * rank + 2 * state + BLOCK) // BLOCK * wide_tiles
-    late_tiles = width // BLOCK * wide_tiles
+    late_tiles, spare_tiles, mid_tiles = small_tiles(width, wide_tiles, rank, state)
+    late_tiles += spare_tiles
 
     def shape(*dims, kind=F32):
         return jax.ShapeDtypeStruct(dims, kind)
 
     vm = pltpu.VMEM
     sum_outs, sum_scratch = [], []
-    for tiles in (early_tiles, mid_tiles, late_tiles):
+    for short, tiles in ((False, early_tiles), (True, mid_tiles), (False, late_tiles)):
         for each, (one, two) in zip(
             chunk_tiles(tiles, rows_count), ((near, far), (far, near))
         ):
@@ -889,7 +944,7 @@
                 vm((one, two, each * BLOCK, 128), BF16),
                 vm((one, two, each * BLOCK, 128), BF16),
                 vm((two, each * BLOCK, 128), BF16),
-                vm((two, each * BLOCK, 128), BF16),
+                vm(((two, two) if short else (two,)) + (each * BLOCK, 128), BF16),
             ]
     outs = [
         shape(half_slots, width, kind=BF16),
@@ -933,6 +988,7 @@
         vm((padded // BLOCK, 64, BLOCK), F32),
         vm((128, 1024), BF16),
         vm((2, padded * 16 + 16, inner_w), BF16),
+        vm((2, 256, inner_w), BF16),
         vm((2, padded, inner_w), F32),
         vm((256, inner_w), BF16),
         vm((256, inner_w), BF16),
@@ -963,9 +1019,9 @@
         vm((far, 8, inner_w), F32),
         pltpu.SemaphoreType.DMA((6,)),
         pltpu.SemaphoreType.DMA((6,)),
-        pltpu.SemaphoreType.DMA((4, 2, near + far - 2)),
-        pltpu.SemaphoreType.DMA((4, 2, near + far - 2)),
-        pltpu.SemaphoreType.DMA((4, 2, near + far - 2)),
+        pltpu.SemaphoreType.DMA((4, 2, 2, max(near, far) - 1)),
+        pltpu.SemaphoreType.DMA((4, 2, 2, max(near, far) - 1)),
+        pltpu.SemaphoreType.DMA((4, 2, 2, max(near, far) - 1)),
         pltpu.SemaphoreType.DMA((2, near + far - 2)),
     ]
     in_vmem = pl.BlockSpec(memory_space=pltpu.VMEM)

time: 66.3 us -> 64.8 us (0.977)
  Pallas kernels: 64.8 us -> 63.4 us
    pallas_call x1, Pallas kernels: 61.6 us -> 60.2 us  [per_device(): pl.pallas_call(functools.partial(block_kernel, sizes), out_shape=outs, in...]
where the time goes in v3:
time: 64.8 us; the launch traced here: 64.7 us
  Pallas kernels  63.4 us (98%)
  between operations  1.31 us (2%)
    pallas_call x1, Pallas kernels, per_device(): pl.pallas_call(functools.partial(block_kernel, sizes), out_shape=outs, in...  60.2 us
    pallas_call x1, Pallas kernels, per_device(): pl.pallas_call(functools.partial(finish_kernel, None), out_shape=outs, in...  3.16 us

profile of v3, /device:TPU:0, one launch (start us, length us, event | category | flops | bytes accessed | tf_op | source)
XLA Modules:
  0.0 64.7 jit_solution(15782975437109745739)
XLA Ops:
  1.3 60.2 %shard_map.245 = (bf16[196,384]{1,0:T(8,128)(2,1)}, bf16[784,384]{1,0:T(8,128)(2,1)}, bf16[4,4,96,128]{3,2,1,0:T(8,128)(2,1)}, bf16[4,4,48,128]{3,2,1,0:T(8,128)...) custom-call(bf16[784,384]{1,0:T(8,128)(2,1)} %bitcast.7, ...), custom_call_target="tpu_custom_call" | custom-call | tf_op jit(solution)/shard_map/pallas_call | solution.py:1030
  61.5 3.2 %shard_map.246 = (bf16[196,384]{1,0:T(8,128)(2,1)}, bf16[784,384]{1,0:T(8,128)(2,1)}, f32[192]{0:T(256)}, f32[2,384,384]{2,1,0:T(8,128)}, f32[2,4,384]{2,1,0:T(4...) custom-call(bf16[4,4,96,128]{3,2,1,0:T(8,128)(2,1)} %get-tuple-eleme, ...), custom_call_target="tpu_custom_call" | custom-call | tf_op jit(solution)/shard_map/pallas_call | solution.py:1072

commit v4 on v3

--- a/solution.py
+++ b/solution.py
@@ -384,11 +384,23 @@
         column = iota((BLOCK, half_full), 1).astype(F32)
         chosen[rows_at(block), :] = jnp.where(place == column, 1.0, 0.0).astype(BF16)
 
-    each_block(pick_rows, 25)
-    picked[...] = dot(chosen[...], hidden[...]).astype(BF16)
-    pl.semaphore_wait(barrier, near + far - 1)
-    send_pick = remote(picked, picked_in, 0)
-    send_pick.start()
+    def some_blocks(body, lower, upper):
+        def step(block, carry):
+            body(block)
+            return carry
+
+        lax.fori_loop(lower, upper, step, 0, unroll=upper - lower)
+
+    half_blocks = (blocks + 1) // 2
+    send_picks = []
+    for index, (lower, upper) in ((0, (0, half_blocks)), (6, (half_blocks, blocks))):
+        some_blocks(pick_rows, lower, upper)
+        rows = pl.ds(lower * BLOCK, (upper - lower) * BLOCK)
+        picked[rows, :] = dot(chosen[rows, :], hidden[...]).astype(BF16)
+        if lower == 0:
+            pl.semaphore_wait(barrier, near + far - 1)
+        send_picks.append(remote(picked.at[rows], picked_in.at[rows], index))
+        send_picks[-1].start()
     send_cot = remote(cot_pair.at[inner], cot_pair.at[inner], 1)
 
     def at_rows(value, r):
@@ -420,8 +432,6 @@
     states[0, 0:16, :] = jnp.zeros((16, inner_w), BF16)
     states[1, padded * 16 : padded * 16 + 16, :] = jnp.zeros((16, inner_w), BF16)
 
-    send_pick.wait()
-    send_cot.start()
     gain = norm_gain[...].reshape(1, width)
 
     def norm_rows(block):
@@ -432,7 +442,11 @@
         inverse[rows, :] = scale
         normed[rows, :] = (held * scale * gain).astype(BF16)
 
-    each_block(norm_rows)
+    send_picks[0].wait()
+    some_blocks(norm_rows, 0, half_blocks)
+    send_picks[1].wait()
+    send_cot.start()
+    some_blocks(norm_rows, half_blocks, blocks)
     px[8 : 8 + padded, :] = dot(normed[...], in_weight[0])
 
     taps = conv_weight[...].astype(F32)
@@ -1017,8 +1031,8 @@
         vm((near, 8, inner_w), F32),
         vm((8, inner_w), F32),
         vm((far, 8, inner_w), F32),
-        pltpu.SemaphoreType.DMA((6,)),
-        pltpu.SemaphoreType.DMA((6,)),
+        pltpu.SemaphoreType.DMA((7,)),
+        pltpu.SemaphoreType.DMA((7,)),
         pltpu.SemaphoreType.DMA((4, 2, 2, max(near, far) - 1)),
         pltpu.SemaphoreType.DMA((4, 2, 2, max(near, far) - 1)),
         pltpu.SemaphoreType.DMA((4, 2, 2, max(near, far) - 1)),

time: 64.8 us -> 64.8 us (level)
  no operation moved by 1% of the time
where the time goes in v4:
time: 64.8 us; the launch traced here: 64.6 us
  Pallas kernels  63.3 us (98%)
  between operations  1.31 us (2%)
    pallas_call x1, Pallas kernels, per_device(): pl.pallas_call(functools.partial(block_kernel, sizes), out_shape=outs, in...  60.2 us
    pallas_call x1, Pallas kernels, per_device(): pl.pallas_call(functools.partial(finish_kernel, None), out_shape=outs, in...  3.16 us

profile of v4, /device:TPU:0, one launch (start us, length us, event | category | flops | bytes accessed | tf_op | source)
XLA Modules:
  0.0 64.6 jit_solution(2964770246727089625)
XLA Ops:
  1.3 60.2 %shard_map.245 = (bf16[196,384]{1,0:T(8,128)(2,1)}, bf16[784,384]{1,0:T(8,128)(2,1)}, bf16[4,4,96,128]{3,2,1,0:T(8,128)(2,1)}, bf16[4,4,48,128]{3,2,1,0:T(8,128)...) custom-call(bf16[784,384]{1,0:T(8,128)(2,1)} %bitcast.7, ...), custom_call_target="tpu_custom_call" | custom-call | tf_op jit(solution)/shard_map/pallas_call | solution.py:1044
  61.5 3.2 %shard_map.246 = (bf16[196,384]{1,0:T(8,128)(2,1)}, bf16[784,384]{1,0:T(8,128)(2,1)}, f32[192]{0:T(256)}, f32[2,384,384]{2,1,0:T(8,128)}, f32[2,4,384]{2,1,0:T(4...) custom-call(bf16[4,4,96,128]{3,2,1,0:T(8,128)(2,1)} %get-tuple-eleme, ...), custom_call_target="tpu_custom_call" | custom-call | tf_op jit(solution)/shard_map/pallas_call | solution.py:1086

commit v5 on v4

--- a/solution.py
+++ b/solution.py
@@ -445,9 +445,9 @@
     send_picks[0].wait()
     some_blocks(norm_rows, 0, half_blocks)
     send_picks[1].wait()
-    send_cot.start()
     some_blocks(norm_rows, half_blocks, blocks)
     px[8 : 8 + padded, :] = dot(normed[...], in_weight[0])
+    send_cot.start()
 
     taps = conv_weight[...].astype(F32)
 

time: 64.8 us -> 64.8 us (level)
  no operation moved by 1% of the time
where the time goes in v5:
time: 64.8 us; the launch traced here: 64.7 us
  Pallas kernels  63.3 us (98%)
  between operations  1.31 us (2%)
    pallas_call x1, Pallas kernels, per_device(): pl.pallas_call(functools.partial(block_kernel, sizes), out_shape=outs, in...  60.2 us
    pallas_call x1, Pallas kernels, per_device(): pl.pallas_call(functools.partial(finish_kernel, None), out_shape=outs, in...  3.16 us

profile of v5, /device:TPU:0, one launch (start us, length us, event | category | flops | bytes accessed | tf_op | source)
XLA Modules:
  0.0 64.7 jit_solution(4189348916063850156)
XLA Ops:
  1.3 60.2 %shard_map.245 = (bf16[196,384]{1,0:T(8,128)(2,1)}, bf16[784,384]{1,0:T(8,128)(2,1)}, bf16[4,4,96,128]{3,2,1,0:T(8,128)(2,1)}, bf16[4,4,48,128]{3,2,1,0:T(8,128)...) custom-call(bf16[784,384]{1,0:T(8,128)(2,1)} %bitcast.7, ...), custom_call_target="tpu_custom_call" | custom-call | tf_op jit(solution)/shard_map/pallas_call | solution.py:1044
  61.5 3.2 %shard_map.246 = (bf16[196,384]{1,0:T(8,128)(2,1)}, bf16[784,384]{1,0:T(8,128)(2,1)}, f32[192]{0:T(256)}, f32[2,384,384]{2,1,0:T(8,128)}, f32[2,4,384]{2,1,0:T(4...) custom-call(bf16[4,4,96,128]{3,2,1,0:T(8,128)(2,1)} %get-tuple-eleme, ...), custom_call_target="tpu_custom_call" | custom-call | tf_op jit(solution)/shard_map/pallas_call | solution.py:1086
